TPU v7x, 32 devices: a whole 2x2x4 slice. The times are simulated.
32 devices in a mesh: parts: 2 (over y), samp: 4 (over x, core), bond: 4 (over z).
Axes of the slice: x: 2, y: 2, z: 4, core: 2. Of those that a mesh axis runs over, the one named last changes fastest.
Arguments:
- env_start: bfloat16 [4096, 4096], P(('parts', 'samp'), 'bond'), parts along dimension 0, may hold values from -6 to 6
- stored_sites: bfloat16 [4, 4, 1024, 4, 4096], P('parts', 'samp', None, None, 'bond'), parts along dimension 0, may hold values from -1 to 1
- slab_order: int32 [4, 4], P('parts'), parts along dimension 0, may hold values from 0 to 3, each once within a row
- chosen: int32 [4096, 2], P(('parts', 'samp')), parts along dimension 0, may hold values from 0 to 3
Outputs:
- probabilities: float32 [4096, 2, 4], P(('parts', 'samp')), parts along dimension 0
- env_final: float32 [4096, 4096], P(('parts', 'samp'), 'bond'), parts along dimension 0
There are 2 independent parts, one for each index of `parts`. A program takes and returns all parts, laid end to end along the dimension named above; each array names one. Nothing has to cross between parts.
Inputs may be any that keep to these rules, and one draw needn't show every extreme that they name: Each row of slab_order names every index of samp once.
All inputs are finite; a program needn't handle non-finite values.
Results may differ from a plain program's by a relative error of at most 0.005.
Values may be sent and summed in bfloat16 or wider, within the bound.
No kernel may reach another device: no remote copies, remote signals or barrier semaphores. Data moves between devices by JAX's collectives and lax.ppermute only.
A program may use at most 192 MiB of HBM per device.

v0:
```python
import jax
import jax.numpy as jnp
from jax import lax
from jax.sharding import PartitionSpec as P

STEPS = 2


epsilon = 1e-06


def order_env(gathered, order):
    samples = gathered.shape[0]
    groups = order.shape[0]
    blocks = gathered.reshape(samples, groups, gathered.shape[1] // groups)
    return jnp.take(blocks, order, axis=1).reshape(samples, gathered.shape[1])


def body(env_start, stored_sites, slab_order, chosen):
    samples = env_start.shape[0]
    outcomes = jnp.arange(stored_sites.shape[3], dtype=jnp.int32)
    gathered = lax.all_gather(env_start, "bond", axis=1, tiled=True)
    bond_width = gathered.shape[1]
    factor = jnp.ones((samples,), jnp.float32)
    prob_list = []
    raw_totals = []
    selectors = []
    selected = None
    for site_index in range(STEPS):
        ordered = order_env(gathered, slab_order[site_index])

        def add_slab(running, portion, offset, ordered=ordered):
            slab_rows = portion.shape[1]
            row_count = portion.shape[0] * slab_rows
            return jnp.dot(
                ordered, portion.reshape(row_count, -1), preferred_element_type=jnp.float32
            )

        initial = jnp.zeros((samples, stored_sites.shape[3] * stored_sites.shape[4]), jnp.float32)
        product = add_slab(
            initial,
            lax.all_gather(stored_sites[site_index], "samp", axis=0, tiled=True),
            jnp.int32(0),
        )
        product = product.reshape(samples, stored_sites.shape[3], stored_sites.shape[4])
        selector = (chosen[:, site_index][:, None] == outcomes[None, :]).astype(jnp.float32)
        selected = jnp.einsum("sn,snc->sc", selector, product)
        raw_totals.append(jnp.sum(product * product, axis=2))
        selectors.append(selector)
        if site_index + 1 < STEPS:
            gathered = lax.all_gather(selected.astype(jnp.bfloat16), "bond", axis=1, tiled=True)
    reduced = lax.psum(tuple(raw_totals), "bond")
    for site_index in range(STEPS):
        totals = reduced[site_index] * (factor * factor)[:, None]
        prob_list.append(totals / jnp.sum(totals, axis=1, keepdims=True))
        chosen_total = jnp.sum(totals * selectors[site_index], axis=1)
        factor = factor * lax.rsqrt(chosen_total / bond_width + epsilon)
    env_final = selected * factor[:, None]
    return (jnp.stack(prob_list, axis=1), env_final)


def solution(mesh):
    return jax.shard_map(
        body,
        mesh=mesh,
        in_specs=(
            P(("parts", "samp"), "bond"),
            P("parts", "samp", None, None, "bond"),
            P("parts", None),
            P(("parts", "samp"), None),
        ),
        out_specs=(P(("parts", "samp"), None, None), P(("parts", "samp"), "bond")),
        check_vma=False,
    )
```

profile of v0, /device:TPU:0, one launch (start us, length us, event | category | flops | bytes accessed | tf_op | source)
XLA Modules:
  0.0 684.0 jit_solution(9484244106667084634)
XLA Ops:
  7.2 0.0 all-gather.7.cloned.1.call-start
  7.2 2.3 copy.28
  9.5 0.0 all-gather.7.cloned.1.call-update
  9.5 0.0 all-gather.11.cloned.1.call-start
  9.6 16.0 %fusion.6 = (bf16[1,1,1024,4,1024]{4,3,2,1,0:T(4,128)(2,1)}, bf16[1,1,1024,4,1024]{4,3,2,1,0:T(4,128)(2,1)}) fusion(bf16[2,1,1024,4,1024]{4,3,2,1,0:T(4,128)(2,1)} %param.7), kind=kLoop, calls=%fused_computation.30 | loop fusion | bytes 33554432 | tf_op jit(solution)/shard_map/slice | solution.py:42
  25.6 9.4 %copy.53 = bf16[1,1,1024,4,1024]{4,2,3,1,0:T(8,128)(2,1)} copy(bf16[1,1,1024,4,1024]{4,3,2,1,0:T(4,128)(2,1)} %get-tuple-element.16) | data formatting | bytes 16777216
  35.0 0.0 all-gather.11.cloned.1.call-update
  35.0 0.0 all-gather.13.cloned.1.call-start
  35.1 9.5 %copy.54 = bf16[1,1,1024,4,1024]{4,2,3,1,0:T(8,128)(2,1)} copy(bf16[1,1,1024,4,1024]{4,3,2,1,0:T(4,128)(2,1)} %get-tuple-element.15) | data formatting | bytes 16777216
  44.6 0.0 copy-start.4
  44.6 0.0 copy-start.2
  44.6 0.0 all-gather.13.cloned.1.call-update
  44.6 0.2 all-gather.9.cloned.1.call-start
  44.9 0.4 copy-done.4
  45.3 0.6 compare_and_fusion
  45.9 0.0 copy-done.2
  45.9 0.0 copy-start
  45.9 0.6 copy-done
  46.5 47.1 %all-gather.7.cloned.1.call-done = bf16[512,4096]{0,1:T(8,128)(2,1)} async-done(((bf16[512,1024]{0,1:T(8,128)(2,1)}), bf16[512,4096]{0,1:T(8,128)(2,1)}) %all-gather.7.cloned.1.call-update) | async-done | bytes 4194320 | tf_op jit(solution)/shard_map/all_gather | solution.py:22
  93.6 6.3 copy.29
  99.9 6.7 gather_fusion
  106.6 5.8 select_bitcast_fusion.1
  112.4 6.9 %copy.30 = bf16[512,4,1024]{0,2,1:T(8,128)(2,1)} copy(bf16[512,4,1024]{2,0,1:T(8,128)(2,1)} %select_bitcast_fusion.1) | data formatting | bytes 8388608 | tf_op jit(solution)/shard_map/jit(_take)/select_n | solution.py:16
  119.3 176.0 %all-gather.11.cloned.1.call-done = bf16[4,1,1024,4,1024]{4,2,3,1,0:T(8,128)(2,1)} async-done(((bf16[1,1,1024,4,1024]{4,2,3,1,0:T(8,128)(2,1)}), bf16[4,1,1024,4,1024]{4,2,3,1,0:T(8,128)(2,1)}) %all-gather.11.cloned.1.call-update) | async-done | bytes 33554448 | tf_op jit(solution)/shard_map/all_gather | solution.py:42
  295.3 42.2 %copy.32 = bf16[4,1,1024,4,1024]{4,3,2,0,1:T(4,128)(2,1)} copy(bf16[4,1,1024,4,1024]{4,2,3,1,0:T(8,128)(2,1)} %all-gather.11.cloned.1.call-done) | data formatting | bytes 67108864 | tf_op jit(solution)/shard_map/all_gather | solution.py:42
  337.5 23.5 %copy.55 = bf16[512,8,4,1024]{3,1,2,0:T(8,128)(2,1)} copy(bf16[512,8,4,1024]{3,2,1,0:T(4,128)(2,1)} %bitcast.47) | data formatting | bytes 67108864
  361.0 43.8 %copy.33 = bf16[4096,4096]{1,0:T(8,128)(2,1)} copy(bf16[4096,4096]{0,1:T(8,128)(2,1)} %bitcast.48) | data formatting | bytes 67108864 | tf_op jit(solution)/shard_map/dot_general | solution.py:35
  404.7 25.2 %multiply_reduce_fusion.2 = (f32[512,4]{0,1:T(4,128)S(1)}, bf16[512,1024]{1,0:T(8,128)(2,1)S(1)}) fusion(f32[512,4]{0,1:T(4,128)S(1)} %fusion.3, bf16[512,4096,1]{0,1,2:T(8,128)(2,1)} %bitcast.55, bf16[4,1024,4096]{2,1,0:T(8,128)(2,1)} %bitcast.52), kind=kOutput, calls=%fused_computation.6 | convolution fusion | flops 17187731456 | bytes 38813696 | tf_op jit(solution)/shard_map/dot_general | solution.py:35
  429.9 1.3 copy.46
  431.2 0.0 all-gather.9.cloned.1.call-update
  431.3 0.5 copy.48
  431.8 66.7 %all-gather.13.cloned.1.call-done = bf16[4,1,1024,4,1024]{4,2,3,1,0:T(8,128)(2,1)} async-done(((bf16[1,1,1024,4,1024]{4,2,3,1,0:T(8,128)(2,1)}), bf16[4,1,1024,4,1024]{4,2,3,1,0:T(8,128)(2,1)}) %all-gather.13.cloned.1.call-update) | async-done | bytes 33554448 | tf_op jit(solution)/shard_map/all_gather | solution.py:42
  498.4 42.2 %copy.38 = bf16[4,1,1024,4,1024]{4,3,2,0,1:T(4,128)(2,1)} copy(bf16[4,1,1024,4,1024]{4,2,3,1,0:T(8,128)(2,1)} %all-gather.13.cloned.1.call-done) | data formatting | bytes 67108864 | tf_op jit(solution)/shard_map/all_gather | solution.py:42
  540.6 23.0 %copy.56 = bf16[512,8,4,1024]{3,1,2,0:T(8,128)(2,1)} copy(bf16[512,8,4,1024]{3,2,1,0:T(4,128)(2,1)} %bitcast.49) | data formatting | bytes 67108864
  563.6 41.1 %copy.39 = bf16[4096,4096]{1,0:T(8,128)(2,1)} copy(bf16[4096,4096]{0,1:T(8,128)(2,1)} %bitcast.50) | data formatting | bytes 67108864 | tf_op jit(solution)/shard_map/dot_general | solution.py:35
  604.7 0.0 all-gather.9.cloned.1.call-done
  604.7 6.3 copy.35
  611.0 0.0 copy-start.3
  611.0 5.0 gather_fusion.1
  615.9 0.0 copy-done.3
  615.9 4.6 select_bitcast_fusion
  620.5 6.2 copy.36
  626.7 24.0 %multiply_reduce_fusion.1 = (f32[512,4]{0,1:T(4,128)S(1)}, bf16[512,4,1024]{2,0,1:T(8,128)(2,1)}) fusion(bf16[512,4096,1]{0,1,2:T(8,128)(2,1)} %bitcast.56, bf16[4,1024,4096]{2,1,0:T(8,128)(2,1)} %bitcast.51), kind=kOutput, calls=%fused_computation.5 | convolution fusion | flops 17186158592 | bytes 41951232 | tf_op jit(solution)/shard_map/dot_general | solution.py:35
  650.7 18.7 %all-reduce = (f32[512,4]{0,1:T(4,128)S(1)}, f32[512,4]{0,1:T(4,128)S(1)}) all-reduce(f32[512,4]{0,1:T(4,128)S(1)} %get-tuple-element.21, f32[512,4]{0,1:T(4,128)S(1)} %get-tuple-element.3), channel_id=1, replica_groups=mesh['parts'=2,'samp'=4,'bond'=4] {'bond'}, use_global_device_ids=true, to_apply=%region_4.6 | all-reduce | flops 4096 | bytes 32768 | tf_op jit(solution)/shard_map/psum | solution.py:52
  669.4 0.0 copy-done.1
  669.5 5.6 fusion
  675.1 1.7 bitcast_multiply_fusion
  676.9 0.6 pad_maximum_fusion
  (11 shorter events, 0.1 us)
Async XLA Ops:
  7.2 86.5 %all-gather.7.cloned.1.call-start = ((), (), s32[]{:S(2)}) async-start(), calls=%async_computation | async-start | bytes 5242880 | tf_op jit(solution)/shard_map/all_gather | solution.py:22
  9.5 285.8 %all-gather.11.cloned.1.call-start = ((), (), s32[]{:S(2)}) async-start(), calls=%async_computation.2 | async-start | bytes 41943040 | tf_op jit(solution)/shard_map/all_gather | solution.py:42
  35.0 463.4 %all-gather.13.cloned.1.call-start = ((), (), s32[]{:S(2)}) async-start(), calls=%async_computation.3 | async-start | bytes 41943040 | tf_op jit(solution)/shard_map/all_gather | solution.py:42
  44.6 0.7 copy-start.4
  44.6 1.3 copy-start.2
  44.6 560.1 %all-gather.9.cloned.1.call-start = ((), (), s32[]{:S(2)}) async-start(), calls=%async_computation.1 | async-start | bytes 5242880 | tf_op jit(solution)/shard_map/all_gather | solution.py:51
  45.9 0.6 copy-start
  611.0 5.0 copy-start.3
  626.7 42.7 %copy-start.1 = (s32[512,1]{0,1:T(1,128)S(1)}, s32[512,1]{0,1:T(1,128)}, u32[]{:S(2)}) copy-start(s32[512,1]{0,1:T(1,128)} %copy-done) | copy-start | bytes 6148
Sparse Core Ops, SparseCore 0:
  10.1 83.4 all-gather.6
  95.2 200.0 all-gather.10
  296.8 201.5 all-gather.12
  500.4 80.7 all-gather.8
where the time goes:
time: 687 us; the launch traced here: 684 us
  local copies, waits for them, and re-layouts  293 us (43%)
  waiting for transfers between devices  290 us (42%)
  matrix products  54.8 us (8%)
  blocking collectives  18.7 us (3%)
  between operations  13.8 us (2%)
  other arithmetic  13.4 us (2%)
    all_gather x2, waiting for transfers between devices, body(): lax.all_gather(stored_sites[site_index], 'samp', axis=0, tiled=True)  243 us
    dot_general x2, local copies, waits for them, and re-layouts, add_slab(): jnp.dot(ordered, portion.reshape(row_count, -1), preferred_element_type=j...  84.8 us
    all_gather x2, local copies, waits for them, and re-layouts, body(): lax.all_gather(stored_sites[site_index], 'samp', axis=0, tiled=True)  84.4 us
    unnamed x15, local copies, waits for them, and re-layouts  68.8 us
    dot_general x2, matrix products, add_slab(): jnp.dot(ordered, portion.reshape(row_count, -1), preferred_element_type=j...  49.2 us
    all_gather x1, waiting for transfers between devices, body(): gathered = lax.all_gather(env_start, 'bond', axis=1, tiled=True)  47.1 us
    psum x1, blocking collectives, body(): reduced = lax.psum(tuple(raw_totals), 'bond')  18.7 us
    slice x1, local copies, waits for them, and re-layouts, body(): stored_sites[site_index]  16 us
  transfers between devices with their start and end apart: 4, of which 3 were waited for; matrix products, arithmetic and copies ran while one was open for 44% of the time, Pallas kernels for 0%

commit v1 on v0

v1 whole, which is shorter than its diff:
```python
import functools

import jax
import jax.numpy as jnp
from jax import lax
from jax.experimental import pallas as pl
from jax.experimental.pallas import tpu as pltpu
from jax.sharding import PartitionSpec as P

epsilon = 1e-06
VMEM_LIMIT = 48 * 2**20
DEDUPE = False


def divisor(extent, most):
    size = min(extent, most)
    while extent % size:
        size -= 1
    return size


def params():
    return pltpu.CompilerParams(vmem_limit_bytes=VMEM_LIMIT)


def outcome_major(stored_sites, site):
    _, _, rows, outcomes, columns = stored_sites.shape
    tile = divisor(rows, 128)

    def kernel(source, target):
        target[...] = jnp.swapaxes(source[0, 0], 0, 1)

    return pl.pallas_call(
        kernel,
        grid=(rows // tile,),
        in_specs=[pl.BlockSpec((1, 1, tile, outcomes, columns), lambda i: (site, 0, i, 0, 0))],
        out_specs=pl.BlockSpec((outcomes, tile, columns), lambda i: (0, i, 0)),
        out_shape=jax.ShapeDtypeStruct((outcomes, rows, columns), stored_sites.dtype),
        compiler_params=params(),
        cost_estimate=pl.CostEstimate(
            flops=0, bytes_accessed=4 * rows * outcomes * columns, transcendentals=0
        ),
    )(stored_sites)


def fetch(sources, code, slot_of, target, sem):
    for at, (ref, index) in enumerate(sources):

        @pl.when(code == at)
        def _(ref=ref, index=index):
            pltpu.make_async_copy(slot_of(ref, index), target, sem).start()


def candidates(refs):
    own, near, far, passed = refs
    return [(own, None), (near, None), (far, 0), (far, 1), (passed, 0), (passed, 1)]


def places_of(wanted, column):
    middle = (column == 1) | (column == 2)
    far = jnp.where(middle, 2, 4) + jnp.where((wanted == 1) | (wanted == 2), 0, 1)
    near = wanted // 2 == column // 2
    return jnp.where(wanted == column, 0, jnp.where(near, 1, far)).astype(jnp.int32)


def gather(block):
    near = lax.ppermute(block, "bond", [(0, 1), (1, 0), (2, 3), (3, 2)])
    both = jnp.stack([block, near])
    far = lax.ppermute(both, "bond", [(1, 2), (2, 1)])
    passed = lax.ppermute(far, "bond", [(0, 1), (1, 0), (2, 3), (3, 2)])
    return block, near, far, passed


def pick(blocks, places, start, rows):
    count = places.shape[0]
    columns = blocks[0].shape[1]
    scalars = jnp.concatenate([places, jnp.reshape(start, (1,)).astype(jnp.int32)])

    def kernel(scalars_ref, own, near, far, passed, target, sems):
        begin = pl.multiple_of(scalars_ref[count], 16)

        def slot_of(ref, index):
            ref = ref if index is None else ref.at[index]
            return ref.at[pl.ds(begin, rows)]

        for slot in range(count):
            fetch(
                candidates((own, near, far, passed)),
                scalars_ref[slot],
                slot_of,
                target.at[slot],
                sems.at[slot],
            )
        for slot in range(count):
            pltpu.make_async_copy(slot_of(own, None), target.at[slot], sems.at[slot]).wait()

    return pl.pallas_call(
        kernel,
        grid_spec=pltpu.PrefetchScalarGridSpec(
            num_scalar_prefetch=1,
            grid=(1,),
            in_specs=[pl.BlockSpec(memory_space=pl.ANY)] * 4,
            out_specs=pl.BlockSpec((count, rows, columns), lambda i, s: (0, 0, 0)),
            scratch_shapes=[pltpu.SemaphoreType.DMA((count,))],
        ),
        out_shape=jax.ShapeDtypeStruct((count, rows, columns), blocks[0].dtype),
        compiler_params=params(),
        cost_estimate=pl.CostEstimate(
            flops=0, bytes_accessed=4 * count * rows * columns, transcendentals=0
        ),
    )(scalars, *blocks)


def partials(blocks, places, other, slabs, column):
    count = places.shape[0]
    rows, depth = blocks[0].shape
    outcomes, _, columns = slabs[0].shape
    quarters = 4 if len(other) == 4 else 1
    if quarters == 4:
        places = jnp.concatenate([places, places_of(jnp.arange(4), column)])

    def kernel(places_ref, *refs):
        mine, refs = refs[:4], refs[4:]
        theirs, refs = refs[: len(other)], refs[len(other) :]
        weights, refs = refs[:count], refs[count:]
        own_out, other_out, left, sems = refs

        @pl.when(pl.program_id(0) == 0)
        def _():
            def block_of(ref, index):
                return ref if index is None else ref.at[index]

            for slot in range(count):
                fetch(
                    candidates(mine),
                    places_ref[slot],
                    block_of,
                    left.at[slot, pl.ds(rows, rows)],
                    sems.at[0, slot],
                )
            if quarters == 1:
                copies = [pltpu.make_async_copy(theirs[0], left.at[:, pl.ds(0, rows)], sems.at[1, 0])]
                copies[0].start()
            else:
                part = rows // quarters
                copies = []
                for q in range(quarters):
                    target = left.at[:, pl.ds(q * part, part)]
                    fetch(
                        candidates(theirs), places_ref[count + q], block_of, target, sems.at[1, q]
                    )
                    copies.append(pltpu.make_async_copy(theirs[0], target, sems.at[1, q]))
            for slot in range(count):
                pltpu.make_async_copy(
                    mine[0], left.at[slot, pl.ds(rows, rows)], sems.at[0, slot]
                ).wait()
            for copy in copies:
                copy.wait()

        total = jnp.dot(left[0], weights[0][0], preferred_element_type=jnp.float32)
        for slot in range(1, count):
            total += jnp.dot(left[slot], weights[slot][0], preferred_element_type=jnp.float32)
        other_out[0] = total[:rows].astype(other_out.dtype)
        own_out[0] = total[rows:]

    result = pl.BlockSpec((1, rows, columns), lambda n, s: (n, 0, 0))
    size = outcomes * columns
    return pl.pallas_call(
        kernel,
        grid_spec=pltpu.PrefetchScalarGridSpec(
            num_scalar_prefetch=1,
            grid=(outcomes,),
            in_specs=[pl.BlockSpec(memory_space=pl.ANY)] * (4 + len(other))
            + [pl.BlockSpec((1, depth, columns), lambda n, s: (n, 0, 0))] * count,
            out_specs=[result, result],
            scratch_shapes=[
                pltpu.VMEM((count, 2 * rows, depth), blocks[0].dtype),
                pltpu.SemaphoreType.DMA((2, 4)),
            ],
        ),
        out_shape=[
            jax.ShapeDtypeStruct((outcomes, rows, columns), jnp.float32),
            jax.ShapeDtypeStruct((outcomes, rows, columns), jnp.bfloat16),
        ],
        compiler_params=params(),
        cost_estimate=pl.CostEstimate(
            flops=4 * count * rows * depth * size,
            bytes_accessed=2 * count * depth * size + 6 * rows * size,
            transcendentals=0,
        ),
    )(places, *blocks, *other, *slabs)


def combine(own, received, chosen, kept):
    outcomes, rows, columns = own.shape
    tile = divisor(rows, 128)

    def kernel(own_ref, received_ref, chosen_ref, selected_ref, totals_ref):
        picked = chosen_ref[...]
        lanes = lax.broadcasted_iota(jnp.int32, (tile, 128), 1)
        selected = jnp.zeros((tile, columns), jnp.float32)
        squares = jnp.zeros((tile, 128), jnp.float32)
        for n in range(outcomes):
            product = own_ref[n] + received_ref[n].astype(jnp.float32)
            selected = jnp.where(picked == n, product, selected)
            norm = jnp.sum(product * product, axis=1, keepdims=True)
            squares = jnp.where(lanes == n, norm, squares)
        selected_ref[...] = selected.astype(selected_ref.dtype)
        totals_ref[...] = squares.T[:8]

    block = pl.BlockSpec((outcomes, tile, columns), lambda i: (0, i, 0))
    selected, totals = pl.pallas_call(
        kernel,
        grid=(rows // tile,),
        in_specs=[block, block, pl.BlockSpec((tile, 1), lambda i: (i, 0))],
        out_specs=[
            pl.BlockSpec((tile, columns), lambda i: (i, 0)),
            pl.BlockSpec((8, tile), lambda i: (0, i)),
        ],
        out_shape=[
            jax.ShapeDtypeStruct((rows, columns), kept),
            jax.ShapeDtypeStruct((8, rows), jnp.float32),
        ],
        compiler_params=params(),
        cost_estimate=pl.CostEstimate(
            flops=4 * outcomes * rows * columns,
            bytes_accessed=8 * outcomes * rows * columns,
            transcendentals=0,
        ),
    )(own, received, chosen)
    return selected, totals[:outcomes]


def body(env_start, stored_sites, slab_order, chosen, *, samp, bond):
    steps = stored_sites.shape[0]
    slab = stored_sites.shape[2]
    samples, width = env_start.shape
    inner = samp // 2
    mine = lax.axis_index("samp")
    half, place = mine // inner, mine % inner
    across = [(i, (i + inner) % samp) for i in range(samp)]
    column = lax.axis_index("bond")

    def inner_perm(shift):
        return [
            (h * inner + i, h * inner + (i + shift) % inner) for h in range(2) for i in range(inner)
        ]

    slabs = []
    for site in range(steps):
        block = outcome_major(stored_sites, site)
        slabs.append(
            [block] + [lax.ppermute(block, "samp", inner_perm(d)) for d in range(1, inner)]
        )

    def order_of(site, which):
        ids = [which * inner + (place - d) % inner for d in range(inner)]
        return jnp.stack([slab_order[site, i] for i in ids])

    chunks = 4
    rows = samples // chunks
    env = [env_start[c * rows : (c + 1) * rows] for c in range(chunks)]
    totals = []
    for site in range(steps):
        last = site + 1 == steps
        own_places = places_of(order_of(site, half), column)
        other_places = places_of(order_of(site, 1 - half), column)
        next_env, site_totals = [], []
        for c in range(chunks):
            blocks = gather(env[c])
            if DEDUPE:
                part = rows // bond
                sent = pick(blocks, other_places, column * part, part)
                other = gather(lax.ppermute(sent, "samp", across))
            else:
                sent = pick(blocks, other_places, 0, rows)
                other = (lax.ppermute(sent, "samp", across),)
            own_part, other_part = partials(blocks, own_places, other, slabs[site], column)
            received = lax.ppermute(other_part, "samp", across)
            selected, squares = combine(
                own_part,
                received,
                chosen[c * rows : (c + 1) * rows, site : site + 1],
                jnp.float32 if last else jnp.bfloat16,
            )
            next_env.append(selected)
            site_totals.append(squares)
        env = next_env
        totals.append(jnp.concatenate(site_totals, axis=1))

    stacked = jnp.stack(totals)
    summed = stacked
    for d in range(1, bond):
        summed = summed + lax.ppermute(stacked, "bond", [(i, (i + d) % bond) for i in range(bond)])
    outcomes = jnp.arange(stored_sites.shape[3], dtype=jnp.int32)
    factor = jnp.ones((1, samples), jnp.float32)
    probabilities = []
    for site in range(steps):
        scaled = summed[site] * (factor * factor)
        probabilities.append(scaled / jnp.sum(scaled, axis=0, keepdims=True))
        selector = chosen[:, site][None, :] == outcomes[:, None]
        chosen_total = jnp.sum(jnp.where(selector, scaled, 0.0), axis=0, keepdims=True)
        factor = factor * lax.rsqrt(chosen_total / (width * bond) + epsilon)
    env_final = jnp.concatenate(env, axis=0) * factor[0][:, None]
    return jnp.stack(probabilities).transpose(2, 0, 1), env_final


def plain_body(env_start, stored_sites, slab_order, chosen):
    samples = env_start.shape[0]
    steps = stored_sites.shape[0]
    slab = stored_sites.shape[2]
    outcomes = jnp.arange(stored_sites.shape[3], dtype=jnp.int32)
    gathered = lax.all_gather(env_start, "bond", axis=1, tiled=True)
    bond_width = gathered.shape[1]
    factor = jnp.ones((samples,), jnp.float32)
    prob_list, raw_totals, selectors = [], [], []
    selected = None
    for site in range(steps):
        ordered = jnp.concatenate(
            [
                lax.dynamic_slice_in_dim(gathered, slab_order[site, i] * slab, slab, axis=1)
                for i in range(slab_order.shape[1])
            ],
            axis=1,
        )
        portion = lax.all_gather(stored_sites[site], "samp", axis=0, tiled=True)
        product = jnp.dot(
            ordered, portion.reshape(bond_width, -1), preferred_element_type=jnp.float32
        )
        product = lax.optimization_barrier(product)
        product = product.reshape(samples, stored_sites.shape[3], stored_sites.shape[4])
        selector = (chosen[:, site][:, None] == outcomes[None, :]).astype(jnp.float32)
        selected = jnp.sum(selector[:, :, None] * product, axis=1)
        raw_totals.append(jnp.sum(product * product, axis=2))
        selectors.append(selector)
        if site + 1 < steps:
            gathered = lax.all_gather(selected.astype(jnp.bfloat16), "bond", axis=1, tiled=True)
    reduced = lax.psum(tuple(raw_totals), "bond")
    for site in range(steps):
        totals = reduced[site] * (factor * factor)[:, None]
        prob_list.append(totals / jnp.sum(totals, axis=1, keepdims=True))
        chosen_total = jnp.sum(totals * selectors[site], axis=1)
        factor = factor * lax.rsqrt(chosen_total / bond_width + epsilon)
    return jnp.stack(prob_list, axis=1), selected * factor[:, None]


def solution(mesh):
    samp, bond = mesh.shape["samp"], mesh.shape["bond"]

    def choose(env_start, stored_sites, slab_order, chosen):
        if stored_sites.shape[2] == env_start.shape[1] and samp == 4 and bond == 4:
            return body(env_start, stored_sites, slab_order, chosen, samp=samp, bond=bond)
        return plain_body(env_start, stored_sites, slab_order, chosen)

    return jax.shard_map(
        choose,
        mesh=mesh,
        in_specs=(
            P(("parts", "samp"), "bond"),
            P("parts", "samp", None, None, "bond"),
            P("parts", None),
            P(("parts", "samp"), None),
        ),
        out_specs=(P(("parts", "samp"), None, None), P(("parts", "samp"), "bond")),
        check_vma=False,
    )
```

time: 687 us -> 411 us (0.60)
  local copies, waits for them, and re-layouts: 293 us -> 17.2 us
  waiting for transfers between devices: 290 us -> 152 us
  Pallas kernels: 0 us -> 122 us
  starting transfers between devices: 0.34 us -> 108 us
  matrix products: 54.8 us -> 0 us
  blocking collectives: 18.7 us -> 0 us
  between operations: 13.8 us -> 1.21 us
    all_gather x4 -> x0, waiting for transfers between devices: 290 us -> none  [the longest x2 243 us: body(): lax.all_gather(stored_sites[site_index], 'samp', axis=0, tiled=True)]
    ppermute x0 -> x45, waiting for transfers between devices: none -> 152 us  [the longest x8 107 us: body(): received = lax.ppermute(other_part, 'samp', across)]
    pallas_call x0 -> x26, Pallas kernels: none -> 122 us  [the longest x8 82.5 us: partials(): pl.pallas_call(kernel, grid_spec=pltpu.PrefetchScalarGridSpec(num_scalar_...]
    ppermute x0 -> x45, starting transfers between devices: none -> 108 us  [the longest x8 64.2 us: gather(): passed = lax.ppermute(far, 'bond', [(0, 1), (1, 0), (2, 3), (3, 2)])]
    dot_general x3 -> x0, local copies, waits for them, and re-layouts: 86.1 us -> none  [the longest x2 84.8 us: add_slab(): jnp.dot(ordered, portion.reshape(row_count, -1), preferred_element_type=j...]
    all_gather x2 -> x0, local copies, waits for them, and re-layouts: 84.4 us -> none  [body(): lax.all_gather(stored_sites[site_index], 'samp', axis=0, tiled=True)]
    dot_general x3 -> x0, matrix products: 54.8 us -> none  [the longest x2 49.2 us: add_slab(): jnp.dot(ordered, portion.reshape(row_count, -1), preferred_element_type=j...]
    unnamed x15 -> x46, local copies, waits for them, and re-layouts: 68.8 us -> 16.2 us
  transfers between devices with their start and end apart: 4 -> 45, of which waited for: 3 -> 19; matrix products, arithmetic and copies ran while one was open for 44% -> 2% of each run, Pallas kernels for 0% -> 27%
where the time goes in v1:
time: 411 us; the launch traced here: 410 us
  waiting for transfers between devices  152 us (37%)
  Pallas kernels  122 us (30%)
  starting transfers between devices  108 us (26%)
  local copies, waits for them, and re-layouts  17.2 us (4%)
  other arithmetic  8.75 us (2%)
    ppermute x8, waiting for transfers between devices, body(): received = lax.ppermute(other_part, 'samp', across)  107 us
    pallas_call x8, Pallas kernels, partials(): pl.pallas_call(kernel, grid_spec=pltpu.PrefetchScalarGridSpec(num_scalar_...  82.5 us
    ppermute x8, starting transfers between devices, gather(): passed = lax.ppermute(far, 'bond', [(0, 1), (1, 0), (2, 3), (3, 2)])  64.2 us
    ppermute x8, waiting for transfers between devices, gather(): passed = lax.ppermute(far, 'bond', [(0, 1), (1, 0), (2, 3), (3, 2)])  20.9 us
    pallas_call x2, Pallas kernels, outcome_major(): pl.pallas_call(kernel, grid=(rows // tile,), in_specs=[pl.BlockSpec((1, 1...  19.4 us
    ppermute x8, waiting for transfers between devices, gather(): near = lax.ppermute(block, 'bond', [(0, 1), (1, 0), (2, 3), (3, 2)])  19.3 us
    unnamed x46, local copies, waits for them, and re-layouts  16.2 us
    ppermute x8, starting transfers between devices, gather(): near = lax.ppermute(block, 'bond', [(0, 1), (1, 0), (2, 3), (3, 2)])  14.6 us
  transfers between devices with their start and end apart: 45, of which 19 were waited for; matrix products, arithmetic and copies ran while one was open for 2% of the time, Pallas kernels for 27%

profile of v1, /device:TPU:0, one launch (start us, length us, event | category | flops | bytes accessed | tf_op | source)
XLA Modules:
  0.0 409.7 jit_solution(11306121880103488896)
XLA Ops:
  0.6 9.7 %shard_map.60.refs_5_ = bf16[4,1024,1024]{2,1,0:T(8,128)(2,1)} custom-call(bf16[2,1,1024,4,1024]{4,3,2,1,0:T(4,128)(2,1)} %source.3), custom_call_target="tpu_custom_call" | custom-call | bytes 16777216 | tf_op jit(solution)/shard_map/pallas_call | solution.py:33
  10.8 9.7 %shard_map.73.refs_5_ = bf16[4,1024,1024]{2,1,0:T(8,128)(2,1)} custom-call(bf16[2,1,1024,4,1024]{4,3,2,1,0:T(4,128)(2,1)} %source.3), custom_call_target="tpu_custom_call" | custom-call | bytes 16777216 | tf_op jit(solution)/shard_map/pallas_call | solution.py:33
  20.9 3.0 collective-permute-start.16
  24.0 1.9 collective-permute-start.6
  25.9 5.1 %collective-permute-done.16.near.refs_1_ = bf16[128,1024]{1,0:T(8,128)(2,1)S(1)} collective-permute-done((bf16[128,1024]{1,0:T(8,128)(2,1)S(1)}, bf16[128,1024]{1,0:T(8,128)(2,1)S(1)}, u32[]{:S(2)}, u32[]{:S(2)}) %collective-permute-start.16) | collective-permute-done | bytes 262176 | tf_op jit(solution)/shard_map/ppermute | solution.py:67
  31.0 2.1 collective-permute-start
  33.1 3.5 collective-permute-done.11.near.refs_1_
  38.1 4.1 collective-permute-done.6.near.refs_1_
  43.8 3.5 collective-permute-done.near.refs_1_
  49.5 17.2 %collective-permute-start.18 = (bf16[2,128,1024]{2,1,0:T(8,128)(2,1)}, bf16[2,128,1024]{2,1,0:T(8,128)(2,1)}, u32[]{:S(2)}, u32[]{:S(2)}) collective-permute-start(bf16[2,128,1024]{2,1,0:T(8,128)(2,1)} %collective-permute-done.17.far.refs_2_), channel_id=1, source_target_pairs={{0,1},{1,0},{2,3},{3,2},{4,5},{5,4},{6,7},{7,6},{8,9},{9,8},{10,11... | collective-permute-start | bytes 1572872 | tf_op jit(solution)/shard_map/ppermute | solution.py:70
  66.8 11.1 %collective-permute-start.13 = (bf16[2,128,1024]{2,1,0:T(8,128)(2,1)}, bf16[2,128,1024]{2,1,0:T(8,128)(2,1)}, u32[]{:S(2)}, u32[]{:S(2)}) collective-permute-start(bf16[2,128,1024]{2,1,0:T(8,128)(2,1)} %collective-permute-done.12.far.refs_2_), channel_id=1, source_target_pairs={{0,1},{1,0},{2,3},{3,2},{4,5},{5,4},{6,7},{7,6},{8,9},{9,8},{10,11... | collective-permute-start | bytes 1572872 | tf_op jit(solution)/shard_map/ppermute | solution.py:70
  78.5 8.0 %collective-permute-start.8 = (bf16[2,128,1024]{2,1,0:T(8,128)(2,1)S(1)}, bf16[2,128,1024]{2,1,0:T(8,128)(2,1)S(1)}, u32[]{:S(2)}, u32[]{:S(2)}) collective-permute-start(bf16[2,128,1024]{2,1,0:T(8,128)(2,1)S(1)} %collective-permute-done.7.far.refs_2_), channel_id=1, source_target_pairs={{0,1},{1,0},{2,3},{3,2},{4,5},{5,4},{6,7},{7,6},{8,9},{9,8},{10,11... | collective-permute-start | bytes 1572872 | tf_op jit(solution)/shard_map/ppermute | solution.py:70
  92.5 6.8 %collective-permute-done.8.passed.refs_3_ = bf16[2,128,1024]{2,1,0:T(8,128)(2,1)S(1)} collective-permute-done((bf16[2,128,1024]{2,1,0:T(8,128)(2,1)S(1)}, bf16[2,128,1024]{2,1,0:T(8,128)(2,1)S(1)}, u32[]{:S(2)}, u32[]{:S(2)}) %collective-permute-start.8) | collective-permute-done | bytes 524320 | tf_op jit(solution)/shard_map/ppermute | solution.py:70
  102.8 5.1 %collective-permute-done.2.passed.refs_3_ = bf16[2,128,1024]{2,1,0:T(8,128)(2,1)S(1)} collective-permute-done((bf16[2,128,1024]{2,1,0:T(8,128)(2,1)S(1)}, bf16[2,128,1024]{2,1,0:T(8,128)(2,1)S(1)}, u32[]{:S(2)}, u32[]{:S(2)}) %collective-permute-start.2) | collective-permute-done | bytes 524320 | tf_op jit(solution)/shard_map/ppermute | solution.py:70
  110.6 11.3 %shard_map.70 = (f32[4,128,1024]{2,1,0:T(8,128)S(1)}, bf16[4,128,1024]{2,1,0:T(8,128)(2,1)}) custom-call(s32[2]{0:T(128)S(1)} %compare_select_fusion.7.places_ref, bf16[128,1024]{1,0:T(8,128)(2,1)S(1)} %get-tuple-element.74.own.refs_0_, bf16[128,1024]{1,0:T(8,128)(2,1)S(1)} %collective-permute-done.16.near.refs_1_, ...), custom_call_target="tpu_custom_call" | custom-call | flops 4294967296 | bytes 19922944 | tf_op jit(solution)/shard_map/pallas_call | solution.py:168
  124.7 11.3 %shard_map.67 = (f32[4,128,1024]{2,1,0:T(8,128)S(1)}, bf16[4,128,1024]{2,1,0:T(8,128)(2,1)}) custom-call(s32[2]{0:T(128)S(1)} %compare_select_fusion.7.places_ref, bf16[128,1024]{1,0:T(8,128)(2,1)S(1)} %get-tuple-element.75.own.refs_0_, bf16[128,1024]{1,0:T(8,128)(2,1)S(1)} %collective-permute-done.11.near.refs_1_, ...), custom_call_target="tpu_custom_call" | custom-call | flops 4294967296 | bytes 19922944 | tf_op jit(solution)/shard_map/pallas_call | solution.py:168
  137.8 10.0 %shard_map.64 = (f32[4,128,1024]{2,1,0:T(8,128)S(1)}, bf16[4,128,1024]{2,1,0:T(8,128)(2,1)}) custom-call(s32[2]{0:T(128)S(1)} %compare_select_fusion.7.places_ref, bf16[128,1024]{1,0:T(8,128)(2,1)S(1)} %get-tuple-element.72.own.refs_0_, bf16[128,1024]{1,0:T(8,128)(2,1)S(1)} %collective-permute-done.6.near.refs_1_, ...), custom_call_target="tpu_custom_call" | custom-call | flops 4294967296 | bytes 19922944 | tf_op jit(solution)/shard_map/pallas_call | solution.py:168
  150.7 10.0 %shard_map.61 = (f32[4,128,1024]{2,1,0:T(8,128)S(1)}, bf16[4,128,1024]{2,1,0:T(8,128)(2,1)}) custom-call(s32[2]{0:T(128)S(1)} %compare_select_fusion.7.places_ref, bf16[128,1024]{1,0:T(8,128)(2,1)S(1)} %get-tuple-element.73.own.refs_0_, bf16[128,1024]{1,0:T(8,128)(2,1)S(1)} %collective-permute-done.near.refs_1_, ...), custom_call_target="tpu_custom_call" | custom-call | flops 4294967296 | bytes 19922944 | tf_op jit(solution)/shard_map/pallas_call | solution.py:168
  164.2 1.7 shard_map.71
  166.0 2.1 collective-permute-start.37
  168.2 14.9 %collective-permute-done.15.received_ref = bf16[4,128,1024]{2,1,0:T(8,128)(2,1)} collective-permute-done((bf16[4,128,1024]{2,1,0:T(8,128)(2,1)}, bf16[4,128,1024]{2,1,0:T(8,128)(2,1)}, u32[]{:S(2)}, u32[]{:S(2)}) %collective-permute-start.15) | collective-permute-done | bytes 1048608 | tf_op jit(solution)/shard_map/ppermute | solution.py:279
  184.6 1.7 shard_map.68
  186.4 1.8 collective-permute-start.32
  188.3 17.2 %collective-permute-done.10.received_ref = bf16[4,128,1024]{2,1,0:T(8,128)(2,1)} collective-permute-done((bf16[4,128,1024]{2,1,0:T(8,128)(2,1)}, bf16[4,128,1024]{2,1,0:T(8,128)(2,1)}, u32[]{:S(2)}, u32[]{:S(2)}) %collective-permute-start.10) | collective-permute-done | bytes 1048608 | tf_op jit(solution)/shard_map/ppermute | solution.py:279
  205.5 1.7 shard_map.65
  207.3 1.8 collective-permute-start.27
  210.0 14.4 %collective-permute-done.5.received_ref = bf16[4,128,1024]{2,1,0:T(8,128)(2,1)} collective-permute-done((bf16[4,128,1024]{2,1,0:T(8,128)(2,1)}, bf16[4,128,1024]{2,1,0:T(8,128)(2,1)}, u32[]{:S(2)}, u32[]{:S(2)}) %collective-permute-start.5) | collective-permute-done | bytes 1048608 | tf_op jit(solution)/shard_map/ppermute | solution.py:279
  227.6 1.8 collective-permute-start.21
  231.0 3.1 collective-permute-done.21.near.refs_1_
  234.8 4.6 %collective-permute-start.39 = (bf16[2,128,1024]{2,1,0:T(8,128)(2,1)S(1)}, bf16[2,128,1024]{2,1,0:T(8,128)(2,1)S(1)}, u32[]{:S(2)}, u32[]{:S(2)}) collective-permute-start(bf16[2,128,1024]{2,1,0:T(8,128)(2,1)S(1)} %collective-permute-done.38.far.refs_2_), channel_id=1, source_target_pairs={{0,1},{1,0},{2,3},{3,2},{4,5},{5,4},{6,7},{7,6},{8,9},{9,8},{10,11... | collective-permute-start | bytes 1572872 | tf_op jit(solution)/shard_map/ppermute | solution.py:70
  239.4 7.1 %collective-permute-start.34 = (bf16[2,128,1024]{2,1,0:T(8,128)(2,1)S(1)}, bf16[2,128,1024]{2,1,0:T(8,128)(2,1)S(1)}, u32[]{:S(2)}, u32[]{:S(2)}) collective-permute-start(bf16[2,128,1024]{2,1,0:T(8,128)(2,1)S(1)} %collective-permute-done.33.far.refs_2_), channel_id=1, source_target_pairs={{0,1},{1,0},{2,3},{3,2},{4,5},{5,4},{6,7},{7,6},{8,9},{9,8},{10,11... | collective-permute-start | bytes 1572872 | tf_op jit(solution)/shard_map/ppermute | solution.py:70
  247.9 9.9 %collective-permute-start.29 = (bf16[2,128,1024]{2,1,0:T(8,128)(2,1)S(1)}, bf16[2,128,1024]{2,1,0:T(8,128)(2,1)S(1)}, u32[]{:S(2)}, u32[]{:S(2)}) collective-permute-start(bf16[2,128,1024]{2,1,0:T(8,128)(2,1)S(1)} %collective-permute-done.28.far.refs_2_), channel_id=1, source_target_pairs={{0,1},{1,0},{2,3},{3,2},{4,5},{5,4},{6,7},{7,6},{8,9},{9,8},{10,11... | collective-permute-start | bytes 1572872 | tf_op jit(solution)/shard_map/ppermute | solution.py:70
  257.8 6.3 %collective-permute-start.23 = (bf16[2,128,1024]{2,1,0:T(8,128)(2,1)S(1)}, bf16[2,128,1024]{2,1,0:T(8,128)(2,1)S(1)}, u32[]{:S(2)}, u32[]{:S(2)}) collective-permute-start(bf16[2,128,1024]{2,1,0:T(8,128)(2,1)S(1)} %collective-permute-done.22.far.refs_2_), channel_id=1, source_target_pairs={{0,1},{1,0},{2,3},{3,2},{4,5},{5,4},{6,7},{7,6},{8,9},{9,8},{10,11... | collective-permute-start | bytes 1572872 | tf_op jit(solution)/shard_map/ppermute | solution.py:70
  269.2 5.5 %collective-permute-done.29.passed.refs_3_ = bf16[2,128,1024]{2,1,0:T(8,128)(2,1)S(1)} collective-permute-done((bf16[2,128,1024]{2,1,0:T(8,128)(2,1)S(1)}, bf16[2,128,1024]{2,1,0:T(8,128)(2,1)S(1)}, u32[]{:S(2)}, u32[]{:S(2)}) %collective-permute-start.29) | collective-permute-done | bytes 524320 | tf_op jit(solution)/shard_map/ppermute | solution.py:70
  277.0 3.5 collective-permute-done.23.passed.refs_3_
  282.7 10.0 %shard_map.83 = (f32[4,128,1024]{2,1,0:T(8,128)S(1)}, bf16[4,128,1024]{2,1,0:T(8,128)(2,1)}) custom-call(s32[2]{0:T(128)S(1)} %compare_select_fusion.3.places_ref, bf16[128,1024]{1,0:T(8,128)(2,1)S(1)} %get-tuple-element.58.own.refs_0_, bf16[128,1024]{1,0:T(8,128)(2,1)S(1)} %collective-permute-done.37.near.refs_1_, ...), custom_call_target="tpu_custom_call" | custom-call | flops 4294967296 | bytes 19922944 | tf_op jit(solution)/shard_map/pallas_call | solution.py:168
  294.5 10.0 %shard_map.80 = (f32[4,128,1024]{2,1,0:T(8,128)S(1)}, bf16[4,128,1024]{2,1,0:T(8,128)(2,1)}) custom-call(s32[2]{0:T(128)S(1)} %compare_select_fusion.3.places_ref, bf16[128,1024]{1,0:T(8,128)(2,1)S(1)} %get-tuple-element.54.own.refs_0_, bf16[128,1024]{1,0:T(8,128)(2,1)S(1)} %collective-permute-done.32.near.refs_1_, ...), custom_call_target="tpu_custom_call" | custom-call | flops 4294967296 | bytes 19922944 | tf_op jit(solution)/shard_map/pallas_call | solution.py:168
  307.3 10.0 %shard_map.77 = (f32[4,128,1024]{2,1,0:T(8,128)S(1)}, bf16[4,128,1024]{2,1,0:T(8,128)(2,1)}) custom-call(s32[2]{0:T(128)S(1)} %compare_select_fusion.3.places_ref, bf16[128,1024]{1,0:T(8,128)(2,1)S(1)} %get-tuple-element.50.own.refs_0_, bf16[128,1024]{1,0:T(8,128)(2,1)S(1)} %collective-permute-done.27.near.refs_1_, ...), custom_call_target="tpu_custom_call" | custom-call | flops 4294967296 | bytes 19922944 | tf_op jit(solution)/shard_map/pallas_call | solution.py:168
  319.2 10.0 %shard_map.74 = (f32[4,128,1024]{2,1,0:T(8,128)S(1)}, bf16[4,128,1024]{2,1,0:T(8,128)(2,1)}) custom-call(s32[2]{0:T(128)S(1)} %compare_select_fusion.3.places_ref, bf16[128,1024]{1,0:T(8,128)(2,1)S(1)} %get-tuple-element.46.own.refs_0_, bf16[128,1024]{1,0:T(8,128)(2,1)S(1)} %collective-permute-done.21.near.refs_1_, ...), custom_call_target="tpu_custom_call" | custom-call | flops 4294967296 | bytes 19922944 | tf_op jit(solution)/shard_map/pallas_call | solution.py:168
  332.5 3.6 collective-permute-done.41.received_ref
  336.7 22.0 %collective-permute-done.36.received_ref = bf16[4,128,1024]{2,1,0:T(8,128)(2,1)} collective-permute-done((bf16[4,128,1024]{2,1,0:T(8,128)(2,1)}, bf16[4,128,1024]{2,1,0:T(8,128)(2,1)}, u32[]{:S(2)}, u32[]{:S(2)}) %collective-permute-start.36) | collective-permute-done | bytes 1048608 | tf_op jit(solution)/shard_map/ppermute | solution.py:279
  358.7 1.7 shard_map.81
  360.5 20.7 %collective-permute-done.31.received_ref = bf16[4,128,1024]{2,1,0:T(8,128)(2,1)} collective-permute-done((bf16[4,128,1024]{2,1,0:T(8,128)(2,1)}, bf16[4,128,1024]{2,1,0:T(8,128)(2,1)}, u32[]{:S(2)}, u32[]{:S(2)}) %collective-permute-start.31) | collective-permute-done | bytes 1048608 | tf_op jit(solution)/shard_map/ppermute | solution.py:279
  381.2 1.8 shard_map.78
  383.0 14.6 %collective-permute-done.26.received_ref = bf16[4,128,1024]{2,1,0:T(8,128)(2,1)} collective-permute-done((bf16[4,128,1024]{2,1,0:T(8,128)(2,1)}, bf16[4,128,1024]{2,1,0:T(8,128)(2,1)}, u32[]{:S(2)}, u32[]{:S(2)}) %collective-permute-start.26) | collective-permute-done | bytes 1048608 | tf_op jit(solution)/shard_map/ppermute | solution.py:279
  397.6 1.7 shard_map.75
  399.4 2.5 collective-permute-start.44
  403.4 3.2 collective-permute-done.43
  (151 shorter events, 64.1 us)
Async XLA Ops:
  10.3 100.3 %collective-permute-start.4 = (bf16[4,1024,1024]{2,1,0:T(8,128)(2,1)}, bf16[4,1024,1024]{2,1,0:T(8,128)(2,1)}, u32[]{:S(2)}, u32[]{:S(2)}) collective-permute-start(bf16[4,1024,1024]{2,1,0:T(8,128)(2,1)} %shard_map.60.refs_5_), channel_id=1, source_target_pairs={{0,4},{4,0},{8,12},{12,8},{1,5},{5,1},{9,13},{13,9},{2,6},{6,2},{1... | collective-permute-start | bytes 25165832 | tf_op jit(solution)/shard_map/ppermute | solution.py:253
  20.5 262.2 %collective-permute-start.25 = (bf16[4,1024,1024]{2,1,0:T(8,128)(2,1)}, bf16[4,1024,1024]{2,1,0:T(8,128)(2,1)}, u32[]{:S(2)}, u32[]{:S(2)}) collective-permute-start(bf16[4,1024,1024]{2,1,0:T(8,128)(2,1)} %shard_map.73.refs_5_), channel_id=1, source_target_pairs={{0,4},{4,0},{8,12},{12,8},{1,5},{5,1},{9,13},{13,9},{2,6},{6,2},{1... | collective-permute-start | bytes 25165832 | tf_op jit(solution)/shard_map/ppermute | solution.py:253
  20.9 10.1 %collective-permute-start.16 = (bf16[128,1024]{1,0:T(8,128)(2,1)S(1)}, bf16[128,1024]{1,0:T(8,128)(2,1)S(1)}, u32[]{:S(2)}, u32[]{:S(2)}) collective-permute-start(bf16[128,1024]{1,0:T(8,128)(2,1)S(1)} %get-tuple-element.74.own.refs_0_), channel_id=1, source_target_pairs={{0,1},{1,0},{2,3},{3,2},{4,5},{5,4},{6,7},{7,6},{8,9},{9,8},{10,11... | collective-permute-start | bytes 786440 | tf_op jit(solution)/shard_map/ppermute | solution.py:67
  23.9 12.7 %collective-permute-start.11 = (bf16[128,1024]{1,0:T(8,128)(2,1)S(1)}, bf16[128,1024]{1,0:T(8,128)(2,1)S(1)}, u32[]{:S(2)}, u32[]{:S(2)}) collective-permute-start(bf16[128,1024]{1,0:T(8,128)(2,1)S(1)} %get-tuple-element.75.own.refs_0_), channel_id=1, source_target_pairs={{0,1},{1,0},{2,3},{3,2},{4,5},{5,4},{6,7},{7,6},{8,9},{9,8},{10,11... | collective-permute-start | bytes 786440 | tf_op jit(solution)/shard_map/ppermute | solution.py:67
  24.0 18.3 %collective-permute-start.6 = (bf16[128,1024]{1,0:T(8,128)(2,1)S(1)}, bf16[128,1024]{1,0:T(8,128)(2,1)S(1)}, u32[]{:S(2)}, u32[]{:S(2)}) collective-permute-start(bf16[128,1024]{1,0:T(8,128)(2,1)S(1)} %get-tuple-element.72.own.refs_0_), channel_id=1, source_target_pairs={{0,1},{1,0},{2,3},{3,2},{4,5},{5,4},{6,7},{7,6},{8,9},{9,8},{10,11... | collective-permute-start | bytes 786440 | tf_op jit(solution)/shard_map/ppermute | solution.py:67
  31.0 16.3 %collective-permute-start = (bf16[128,1024]{1,0:T(8,128)(2,1)S(1)}, bf16[128,1024]{1,0:T(8,128)(2,1)S(1)}, u32[]{:S(2)}, u32[]{:S(2)}) collective-permute-start(bf16[128,1024]{1,0:T(8,128)(2,1)S(1)} %get-tuple-element.73.own.refs_0_), channel_id=1, source_target_pairs={{0,1},{1,0},{2,3},{3,2},{4,5},{5,4},{6,7},{7,6},{8,9},{9,8},{10,11... | collective-permute-start | bytes 786440 | tf_op jit(solution)/shard_map/ppermute | solution.py:67
  33.0 44.8 %copy-start.18 = (s32[2,4]{1,0:T(2,128)S(1)}, s32[2,4]{1,0:T(2,128)}, u32[]{:S(2)}) copy-start(s32[2,4]{1,0:T(2,128)} %param.6) | copy-start | bytes 100
  36.6 12.2 %collective-permute-start.17 = (bf16[2,128,1024]{2,1,0:T(8,128)(2,1)S(1)}, bf16[2,128,1024]{2,1,0:T(8,128)(2,1)}, u32[]{:S(2)}, u32[]{:S(2)}) collective-permute-start(bf16[2,128,1024]{2,1,0:T(8,128)(2,1)S(1)} %pad_maximum_fusion.3), channel_id=1, source_target_pairs={{1,2},{2,1},{5,6},{6,5},{9,10},{10,9},{13,14},{14,13},{17,18},{18,... | collective-permute-start | bytes 1572872 | tf_op jit(solution)/shard_map/ppermute | solution.py:69
  42.2 7.3 %collective-permute-start.12 = (bf16[2,128,1024]{2,1,0:T(8,128)(2,1)S(1)}, bf16[2,128,1024]{2,1,0:T(8,128)(2,1)}, u32[]{:S(2)}, u32[]{:S(2)}) collective-permute-start(bf16[2,128,1024]{2,1,0:T(8,128)(2,1)S(1)} %pad_maximum_fusion.2), channel_id=1, source_target_pairs={{1,2},{2,1},{5,6},{6,5},{9,10},{10,9},{13,14},{14,13},{17,18},{18,... | collective-permute-start | bytes 1572872 | tf_op jit(solution)/shard_map/ppermute | solution.py:69
  47.3 19.4 %collective-permute-start.7 = (bf16[2,128,1024]{2,1,0:T(8,128)(2,1)S(1)}, bf16[2,128,1024]{2,1,0:T(8,128)(2,1)S(1)}, u32[]{:S(2)}, u32[]{:S(2)}) collective-permute-start(bf16[2,128,1024]{2,1,0:T(8,128)(2,1)S(1)} %pad_maximum_fusion.1), channel_id=1, source_target_pairs={{1,2},{2,1},{5,6},{6,5},{9,10},{10,9},{13,14},{14,13},{17,18},{18,... | collective-permute-start | bytes 1572872 | tf_op jit(solution)/shard_map/ppermute | solution.py:69
  48.8 29.7 %collective-permute-start.1 = (bf16[2,128,1024]{2,1,0:T(8,128)(2,1)}, bf16[2,128,1024]{2,1,0:T(8,128)(2,1)S(1)}, u32[]{:S(2)}, u32[]{:S(2)}) collective-permute-start(bf16[2,128,1024]{2,1,0:T(8,128)(2,1)} %pad_maximum_fusion), channel_id=1, source_target_pairs={{1,2},{2,1},{5,6},{6,5},{9,10},{10,9},{13,14},{14,13},{17,18},{18,... | collective-permute-start | bytes 1572872 | tf_op jit(solution)/shard_map/ppermute | solution.py:69
  49.5 38.3 %collective-permute-start.18 = (bf16[2,128,1024]{2,1,0:T(8,128)(2,1)}, bf16[2,128,1024]{2,1,0:T(8,128)(2,1)}, u32[]{:S(2)}, u32[]{:S(2)}) collective-permute-start(bf16[2,128,1024]{2,1,0:T(8,128)(2,1)} %collective-permute-done.17.far.refs_2_), channel_id=1, source_target_pairs={{0,1},{1,0},{2,3},{3,2},{4,5},{5,4},{6,7},{7,6},{8,9},{9,8},{10,11... | collective-permute-start | bytes 1572872 | tf_op jit(solution)/shard_map/ppermute | solution.py:70
  66.8 22.6 %collective-permute-start.13 = (bf16[2,128,1024]{2,1,0:T(8,128)(2,1)}, bf16[2,128,1024]{2,1,0:T(8,128)(2,1)}, u32[]{:S(2)}, u32[]{:S(2)}) collective-permute-start(bf16[2,128,1024]{2,1,0:T(8,128)(2,1)} %collective-permute-done.12.far.refs_2_), channel_id=1, source_target_pairs={{0,1},{1,0},{2,3},{3,2},{4,5},{5,4},{6,7},{7,6},{8,9},{9,8},{10,11... | collective-permute-start | bytes 1572872 | tf_op jit(solution)/shard_map/ppermute | solution.py:70
  78.5 20.8 %collective-permute-start.8 = (bf16[2,128,1024]{2,1,0:T(8,128)(2,1)S(1)}, bf16[2,128,1024]{2,1,0:T(8,128)(2,1)S(1)}, u32[]{:S(2)}, u32[]{:S(2)}) collective-permute-start(bf16[2,128,1024]{2,1,0:T(8,128)(2,1)S(1)} %collective-permute-done.7.far.refs_2_), channel_id=1, source_target_pairs={{0,1},{1,0},{2,3},{3,2},{4,5},{5,4},{6,7},{7,6},{8,9},{9,8},{10,11... | collective-permute-start | bytes 1572872 | tf_op jit(solution)/shard_map/ppermute | solution.py:70
  87.8 20.0 %collective-permute-start.2 = (bf16[2,128,1024]{2,1,0:T(8,128)(2,1)S(1)}, bf16[2,128,1024]{2,1,0:T(8,128)(2,1)S(1)}, u32[]{:S(2)}, u32[]{:S(2)}) collective-permute-start(bf16[2,128,1024]{2,1,0:T(8,128)(2,1)S(1)} %collective-permute-done.1.far.refs_2_), channel_id=1, source_target_pairs={{0,1},{1,0},{2,3},{3,2},{4,5},{5,4},{6,7},{7,6},{8,9},{9,8},{10,11... | collective-permute-start | bytes 1572872 | tf_op jit(solution)/shard_map/ppermute | solution.py:70
  89.4 20.6 %collective-permute-start.19 = (bf16[2,128,1024]{2,1,0:T(8,128)(2,1)S(1)}, bf16[2,128,1024]{2,1,0:T(8,128)(2,1)S(1)}, u32[]{:S(2)}, u32[]{:S(2)}) collective-permute-start(bf16[2,128,1024]{2,1,0:T(8,128)(2,1)S(1)} %shard_map.69), channel_id=1, source_target_pairs={{0,8},{4,12},{8,0},{12,4},{1,9},{5,13},{9,1},{13,5},{2,10},{6,14},... | collective-permute-start | bytes 1572872 | tf_op jit(solution)/shard_map/ppermute | solution.py:277
  99.3 25.4 %collective-permute-start.14 = (bf16[2,128,1024]{2,1,0:T(8,128)(2,1)S(1)}, bf16[2,128,1024]{2,1,0:T(8,128)(2,1)S(1)}, u32[]{:S(2)}, u32[]{:S(2)}) collective-permute-start(bf16[2,128,1024]{2,1,0:T(8,128)(2,1)S(1)} %shard_map.66), channel_id=1, source_target_pairs={{0,8},{4,12},{8,0},{12,4},{1,9},{5,13},{9,1},{13,5},{2,10},{6,14},... | collective-permute-start | bytes 1572872 | tf_op jit(solution)/shard_map/ppermute | solution.py:277
  107.8 30.0 %collective-permute-start.9 = (bf16[2,128,1024]{2,1,0:T(8,128)(2,1)S(1)}, bf16[2,128,1024]{2,1,0:T(8,128)(2,1)S(1)}, u32[]{:S(2)}, u32[]{:S(2)}) collective-permute-start(bf16[2,128,1024]{2,1,0:T(8,128)(2,1)S(1)} %shard_map.63), channel_id=1, source_target_pairs={{0,8},{4,12},{8,0},{12,4},{1,9},{5,13},{9,1},{13,5},{2,10},{6,14},... | collective-permute-start | bytes 1572872 | tf_op jit(solution)/shard_map/ppermute | solution.py:277
  110.0 40.7 %collective-permute-start.3 = (bf16[2,128,1024]{2,1,0:T(8,128)(2,1)S(1)}, bf16[2,128,1024]{2,1,0:T(8,128)(2,1)S(1)}, u32[]{:S(2)}, u32[]{:S(2)}) collective-permute-start(bf16[2,128,1024]{2,1,0:T(8,128)(2,1)S(1)} %shard_map.59), channel_id=1, source_target_pairs={{0,8},{4,12},{8,0},{12,4},{1,9},{5,13},{9,1},{13,5},{2,10},{6,14},... | collective-permute-start | bytes 1572872 | tf_op jit(solution)/shard_map/ppermute | solution.py:277
  123.2 39.4 %collective-permute-start.20 = (bf16[4,128,1024]{2,1,0:T(8,128)(2,1)}, bf16[4,128,1024]{2,1,0:T(8,128)(2,1)}, u32[]{:S(2)}, u32[]{:S(2)}) collective-permute-start(bf16[4,128,1024]{2,1,0:T(8,128)(2,1)} %get-tuple-element.44), channel_id=1, source_target_pairs={{0,8},{4,12},{8,0},{12,4},{1,9},{5,13},{9,1},{13,5},{2,10},{6,14},... | collective-permute-start | bytes 3145736 | tf_op jit(solution)/shard_map/ppermute | solution.py:279
  137.3 45.8 %collective-permute-start.15 = (bf16[4,128,1024]{2,1,0:T(8,128)(2,1)}, bf16[4,128,1024]{2,1,0:T(8,128)(2,1)}, u32[]{:S(2)}, u32[]{:S(2)}) collective-permute-start(bf16[4,128,1024]{2,1,0:T(8,128)(2,1)} %get-tuple-element.41), channel_id=1, source_target_pairs={{0,8},{4,12},{8,0},{12,4},{1,9},{5,13},{9,1},{13,5},{2,10},{6,14},... | collective-permute-start | bytes 3145736 | tf_op jit(solution)/shard_map/ppermute | solution.py:279
  149.2 56.3 %collective-permute-start.10 = (bf16[4,128,1024]{2,1,0:T(8,128)(2,1)}, bf16[4,128,1024]{2,1,0:T(8,128)(2,1)}, u32[]{:S(2)}, u32[]{:S(2)}) collective-permute-start(bf16[4,128,1024]{2,1,0:T(8,128)(2,1)} %get-tuple-element.38), channel_id=1, source_target_pairs={{0,8},{4,12},{8,0},{12,4},{1,9},{5,13},{9,1},{13,5},{2,10},{6,14},... | collective-permute-start | bytes 3145736 | tf_op jit(solution)/shard_map/ppermute | solution.py:279
  162.0 62.3 %collective-permute-start.5 = (bf16[4,128,1024]{2,1,0:T(8,128)(2,1)}, bf16[4,128,1024]{2,1,0:T(8,128)(2,1)}, u32[]{:S(2)}, u32[]{:S(2)}) collective-permute-start(bf16[4,128,1024]{2,1,0:T(8,128)(2,1)} %get-tuple-element.35), channel_id=1, source_target_pairs={{0,8},{4,12},{8,0},{12,4},{1,9},{5,13},{9,1},{13,5},{2,10},{6,14},... | collective-permute-start | bytes 3145736 | tf_op jit(solution)/shard_map/ppermute | solution.py:279
  166.0 39.6 %copy-start.9 = (f32[4,128,1024]{2,1,0:T(8,128)S(1)}, f32[4,128,1024]{2,1,0:T(8,128)}, u32[]{:S(2)}) copy-start(f32[4,128,1024]{2,1,0:T(8,128)} %copy-done.8) | copy-start | bytes 6291460
  166.0 43.1 %collective-permute-start.37 = (bf16[128,1024]{1,0:T(8,128)(2,1)S(1)}, bf16[128,1024]{1,0:T(8,128)(2,1)S(1)}, u32[]{:S(2)}, u32[]{:S(2)}) collective-permute-start(bf16[128,1024]{1,0:T(8,128)(2,1)S(1)} %get-tuple-element.58.own.refs_0_), channel_id=1, source_target_pairs={{0,1},{1,0},{2,3},{3,2},{4,5},{5,4},{6,7},{7,6},{8,9},{9,8},{10,11... | collective-permute-start | bytes 786440 | tf_op jit(solution)/shard_map/ppermute | solution.py:67
  186.4 43.1 %collective-permute-start.32 = (bf16[128,1024]{1,0:T(8,128)(2,1)S(1)}, bf16[128,1024]{1,0:T(8,128)(2,1)S(1)}, u32[]{:S(2)}, u32[]{:S(2)}) collective-permute-start(bf16[128,1024]{1,0:T(8,128)(2,1)S(1)} %get-tuple-element.54.own.refs_0_), channel_id=1, source_target_pairs={{0,1},{1,0},{2,3},{3,2},{4,5},{5,4},{6,7},{7,6},{8,9},{9,8},{10,11... | collective-permute-start | bytes 786440 | tf_op jit(solution)/shard_map/ppermute | solution.py:67
  207.3 22.9 %collective-permute-start.27 = (bf16[128,1024]{1,0:T(8,128)(2,1)S(1)}, bf16[128,1024]{1,0:T(8,128)(2,1)S(1)}, u32[]{:S(2)}, u32[]{:S(2)}) collective-permute-start(bf16[128,1024]{1,0:T(8,128)(2,1)S(1)} %get-tuple-element.50.own.refs_0_), channel_id=1, source_target_pairs={{0,1},{1,0},{2,3},{3,2},{4,5},{5,4},{6,7},{7,6},{8,9},{9,8},{10,11... | collective-permute-start | bytes 786440 | tf_op jit(solution)/shard_map/ppermute | solution.py:67
  209.1 25.7 %collective-permute-start.38 = (bf16[2,128,1024]{2,1,0:T(8,128)(2,1)S(1)}, bf16[2,128,1024]{2,1,0:T(8,128)(2,1)S(1)}, u32[]{:S(2)}, u32[]{:S(2)}) collective-permute-start(bf16[2,128,1024]{2,1,0:T(8,128)(2,1)S(1)} %pad_maximum_fusion.7), channel_id=1, source_target_pairs={{1,2},{2,1},{5,6},{6,5},{9,10},{10,9},{13,14},{14,13},{17,18},{18,... | collective-permute-start | bytes 1572872 | tf_op jit(solution)/shard_map/ppermute | solution.py:69
  227.6 6.4 %collective-permute-start.21 = (bf16[128,1024]{1,0:T(8,128)(2,1)S(1)}, bf16[128,1024]{1,0:T(8,128)(2,1)S(1)}, u32[]{:S(2)}, u32[]{:S(2)}) collective-permute-start(bf16[128,1024]{1,0:T(8,128)(2,1)S(1)} %get-tuple-element.46.own.refs_0_), channel_id=1, source_target_pairs={{0,1},{1,0},{2,3},{3,2},{4,5},{5,4},{6,7},{7,6},{8,9},{9,8},{10,11... | collective-permute-start | bytes 786440 | tf_op jit(solution)/shard_map/ppermute | solution.py:67
  229.5 9.9 %collective-permute-start.33 = (bf16[2,128,1024]{2,1,0:T(8,128)(2,1)S(1)}, bf16[2,128,1024]{2,1,0:T(8,128)(2,1)S(1)}, u32[]{:S(2)}, u32[]{:S(2)}) collective-permute-start(bf16[2,128,1024]{2,1,0:T(8,128)(2,1)S(1)} %pad_maximum_fusion.6), channel_id=1, source_target_pairs={{1,2},{2,1},{5,6},{6,5},{9,10},{10,9},{13,14},{14,13},{17,18},{18,... | collective-permute-start | bytes 1572872 | tf_op jit(solution)/shard_map/ppermute | solution.py:69
  230.3 17.6 %collective-permute-start.28 = (bf16[2,128,1024]{2,1,0:T(8,128)(2,1)S(1)}, bf16[2,128,1024]{2,1,0:T(8,128)(2,1)S(1)}, u32[]{:S(2)}, u32[]{:S(2)}) collective-permute-start(bf16[2,128,1024]{2,1,0:T(8,128)(2,1)S(1)} %pad_maximum_fusion.5), channel_id=1, source_target_pairs={{1,2},{2,1},{5,6},{6,5},{9,10},{10,9},{13,14},{14,13},{17,18},{18,... | collective-permute-start | bytes 1572872 | tf_op jit(solution)/shard_map/ppermute | solution.py:69
  234.1 23.6 %collective-permute-start.22 = (bf16[2,128,1024]{2,1,0:T(8,128)(2,1)S(1)}, bf16[2,128,1024]{2,1,0:T(8,128)(2,1)S(1)}, u32[]{:S(2)}, u32[]{:S(2)}) collective-permute-start(bf16[2,128,1024]{2,1,0:T(8,128)(2,1)S(1)} %pad_maximum_fusion.4), channel_id=1, source_target_pairs={{1,2},{2,1},{5,6},{6,5},{9,10},{10,9},{13,14},{14,13},{17,18},{18,... | collective-permute-start | bytes 1572872 | tf_op jit(solution)/shard_map/ppermute | solution.py:69
  234.8 29.4 %collective-permute-start.39 = (bf16[2,128,1024]{2,1,0:T(8,128)(2,1)S(1)}, bf16[2,128,1024]{2,1,0:T(8,128)(2,1)S(1)}, u32[]{:S(2)}, u32[]{:S(2)}) collective-permute-start(bf16[2,128,1024]{2,1,0:T(8,128)(2,1)S(1)} %collective-permute-done.38.far.refs_2_), channel_id=1, source_target_pairs={{0,1},{1,0},{2,3},{3,2},{4,5},{5,4},{6,7},{7,6},{8,9},{9,8},{10,11... | collective-permute-start | bytes 1572872 | tf_op jit(solution)/shard_map/ppermute | solution.py:70
  239.4 27.2 %collective-permute-start.34 = (bf16[2,128,1024]{2,1,0:T(8,128)(2,1)S(1)}, bf16[2,128,1024]{2,1,0:T(8,128)(2,1)S(1)}, u32[]{:S(2)}, u32[]{:S(2)}) collective-permute-start(bf16[2,128,1024]{2,1,0:T(8,128)(2,1)S(1)} %collective-permute-done.33.far.refs_2_), channel_id=1, source_target_pairs={{0,1},{1,0},{2,3},{3,2},{4,5},{5,4},{6,7},{7,6},{8,9},{9,8},{10,11... | collective-permute-start | bytes 1572872 | tf_op jit(solution)/shard_map/ppermute | solution.py:70
  247.9 26.8 %collective-permute-start.29 = (bf16[2,128,1024]{2,1,0:T(8,128)(2,1)S(1)}, bf16[2,128,1024]{2,1,0:T(8,128)(2,1)S(1)}, u32[]{:S(2)}, u32[]{:S(2)}) collective-permute-start(bf16[2,128,1024]{2,1,0:T(8,128)(2,1)S(1)} %collective-permute-done.28.far.refs_2_), channel_id=1, source_target_pairs={{0,1},{1,0},{2,3},{3,2},{4,5},{5,4},{6,7},{7,6},{8,9},{9,8},{10,11... | collective-permute-start | bytes 1572872 | tf_op jit(solution)/shard_map/ppermute | solution.py:70
  257.8 22.7 %collective-permute-start.23 = (bf16[2,128,1024]{2,1,0:T(8,128)(2,1)S(1)}, bf16[2,128,1024]{2,1,0:T(8,128)(2,1)S(1)}, u32[]{:S(2)}, u32[]{:S(2)}) collective-permute-start(bf16[2,128,1024]{2,1,0:T(8,128)(2,1)S(1)} %collective-permute-done.22.far.refs_2_), channel_id=1, source_target_pairs={{0,1},{1,0},{2,3},{3,2},{4,5},{5,4},{6,7},{7,6},{8,9},{9,8},{10,11... | collective-permute-start | bytes 1572872 | tf_op jit(solution)/shard_map/ppermute | solution.py:70
  265.1 17.6 %collective-permute-start.40 = (bf16[2,128,1024]{2,1,0:T(8,128)(2,1)S(1)}, bf16[2,128,1024]{2,1,0:T(8,128)(2,1)S(1)}, u32[]{:S(2)}, u32[]{:S(2)}) collective-permute-start(bf16[2,128,1024]{2,1,0:T(8,128)(2,1)S(1)} %shard_map.82), channel_id=1, source_target_pairs={{0,8},{4,12},{8,0},{12,4},{1,9},{5,13},{9,1},{13,5},{2,10},{6,14},... | collective-permute-start | bytes 1572872 | tf_op jit(solution)/shard_map/ppermute | solution.py:277
  267.3 27.2 %collective-permute-start.35 = (bf16[2,128,1024]{2,1,0:T(8,128)(2,1)S(1)}, bf16[2,128,1024]{2,1,0:T(8,128)(2,1)S(1)}, u32[]{:S(2)}, u32[]{:S(2)}) collective-permute-start(bf16[2,128,1024]{2,1,0:T(8,128)(2,1)S(1)} %shard_map.79), channel_id=1, source_target_pairs={{0,8},{4,12},{8,0},{12,4},{1,9},{5,13},{9,1},{13,5},{2,10},{6,14},... | collective-permute-start | bytes 1572872 | tf_op jit(solution)/shard_map/ppermute | solution.py:277
  275.4 32.0 %collective-permute-start.30 = (bf16[2,128,1024]{2,1,0:T(8,128)(2,1)S(1)}, bf16[2,128,1024]{2,1,0:T(8,128)(2,1)S(1)}, u32[]{:S(2)}, u32[]{:S(2)}) collective-permute-start(bf16[2,128,1024]{2,1,0:T(8,128)(2,1)S(1)} %shard_map.76), channel_id=1, source_target_pairs={{0,8},{4,12},{8,0},{12,4},{1,9},{5,13},{9,1},{13,5},{2,10},{6,14},... | collective-permute-start | bytes 1572872 | tf_op jit(solution)/shard_map/ppermute | solution.py:277
  281.1 38.1 %collective-permute-start.24 = (bf16[2,128,1024]{2,1,0:T(8,128)(2,1)S(1)}, bf16[2,128,1024]{2,1,0:T(8,128)(2,1)S(1)}, u32[]{:S(2)}, u32[]{:S(2)}) collective-permute-start(bf16[2,128,1024]{2,1,0:T(8,128)(2,1)S(1)} %shard_map.72), channel_id=1, source_target_pairs={{0,8},{4,12},{8,0},{12,4},{1,9},{5,13},{9,1},{13,5},{2,10},{6,14},... | collective-permute-start | bytes 1572872 | tf_op jit(solution)/shard_map/ppermute | solution.py:277
  294.0 42.1 %collective-permute-start.41 = (bf16[4,128,1024]{2,1,0:T(8,128)(2,1)}, bf16[4,128,1024]{2,1,0:T(8,128)(2,1)S(1)}, u32[]{:S(2)}, u32[]{:S(2)}) collective-permute-start(bf16[4,128,1024]{2,1,0:T(8,128)(2,1)} %get-tuple-element.60), channel_id=1, source_target_pairs={{0,8},{4,12},{8,0},{12,4},{1,9},{5,13},{9,1},{13,5},{2,10},{6,14},... | collective-permute-start | bytes 3145736 | tf_op jit(solution)/shard_map/ppermute | solution.py:279
  305.8 52.9 %collective-permute-start.36 = (bf16[4,128,1024]{2,1,0:T(8,128)(2,1)}, bf16[4,128,1024]{2,1,0:T(8,128)(2,1)}, u32[]{:S(2)}, u32[]{:S(2)}) collective-permute-start(bf16[4,128,1024]{2,1,0:T(8,128)(2,1)} %get-tuple-element.56), channel_id=1, source_target_pairs={{0,8},{4,12},{8,0},{12,4},{1,9},{5,13},{9,1},{13,5},{2,10},{6,14},... | collective-permute-start | bytes 3145736 | tf_op jit(solution)/shard_map/ppermute | solution.py:279
  318.7 62.5 %collective-permute-start.31 = (bf16[4,128,1024]{2,1,0:T(8,128)(2,1)}, bf16[4,128,1024]{2,1,0:T(8,128)(2,1)}, u32[]{:S(2)}, u32[]{:S(2)}) collective-permute-start(bf16[4,128,1024]{2,1,0:T(8,128)(2,1)} %get-tuple-element.52), channel_id=1, source_target_pairs={{0,8},{4,12},{8,0},{12,4},{1,9},{5,13},{9,1},{13,5},{2,10},{6,14},... | collective-permute-start | bytes 3145736 | tf_op jit(solution)/shard_map/ppermute | solution.py:279
  330.5 67.1 %collective-permute-start.26 = (bf16[4,128,1024]{2,1,0:T(8,128)(2,1)}, bf16[4,128,1024]{2,1,0:T(8,128)(2,1)}, u32[]{:S(2)}, u32[]{:S(2)}) collective-permute-start(bf16[4,128,1024]{2,1,0:T(8,128)(2,1)} %get-tuple-element.48), channel_id=1, source_target_pairs={{0,8},{4,12},{8,0},{12,4},{1,9},{5,13},{9,1},{13,5},{2,10},{6,14},... | collective-permute-start | bytes 3145736 | tf_op jit(solution)/shard_map/ppermute | solution.py:279
  336.7 44.5 %copy-start.7 = (f32[4,128,1024]{2,1,0:T(8,128)S(1)}, f32[4,128,1024]{2,1,0:T(8,128)}, u32[]{:S(2)}) copy-start(f32[4,128,1024]{2,1,0:T(8,128)} %copy-done.6) | copy-start | bytes 6291460
  399.4 4.0 collective-permute-start.44
  401.9 4.6 %collective-permute-start.43 = (f32[2,4,512]{2,1,0:T(4,128)S(1)}, f32[2,4,512]{2,1,0:T(4,128)S(1)}, u32[]{:S(2)}, u32[]{:S(2)}) collective-permute-start(f32[2,4,512]{2,1,0:T(4,128)S(1)} %pad_maximum_fusion.8), channel_id=1, source_target_pairs={{0,2},{1,3},{2,0},{3,1},{4,6},{5,7},{6,4},{7,5},{8,10},{9,11},{10,... | collective-permute-start | bytes 49160 | tf_op jit(solution)/shard_map/ppermute | solution.py:294
  401.9 5.5 %collective-permute-start.42 = (f32[2,4,512]{2,1,0:T(4,128)S(1)}, f32[2,4,512]{2,1,0:T(4,128)S(1)}, u32[]{:S(2)}, u32[]{:S(2)}) collective-permute-start(f32[2,4,512]{2,1,0:T(4,128)S(1)} %pad_maximum_fusion.8), channel_id=1, source_target_pairs={{0,1},{1,2},{2,3},{3,0},{4,5},{5,6},{6,7},{7,4},{8,9},{9,10},{10,1... | collective-permute-start | bytes 49160 | tf_op jit(solution)/shard_map/ppermute | solution.py:294
  (16 other events, 119.8 us)

commit v2 on v1

v2 whole, which is shorter than its diff:
```python
import functools

import jax
import jax.numpy as jnp
from jax import lax
from jax.experimental import pallas as pl
from jax.experimental.pallas import tpu as pltpu
from jax.sharding import PartitionSpec as P

epsilon = 1e-06
VMEM_LIMIT = 48 * 2**20
COST = 10.0
CHUNKS = 4


def divisor(extent, most):
    size = min(extent, most)
    while extent % size:
        size -= 1
    return size


def params():
    return pltpu.CompilerParams(vmem_limit_bytes=VMEM_LIMIT)


ANY = pl.BlockSpec(memory_space=pl.ANY)


def cost(flops, moved):
    return pl.CostEstimate(
        flops=int(COST * flops), bytes_accessed=int(COST * moved), transcendentals=0
    )


def outcome_major(stored_sites, site, after=()):
    _, _, rows, outcomes, columns = stored_sites.shape
    tile = divisor(rows, 128)

    def kernel(source, *refs):
        refs[-1][...] = jnp.swapaxes(source[0, 0], 0, 1)

    return pl.pallas_call(
        kernel,
        grid=(rows // tile,),
        in_specs=[pl.BlockSpec((1, 1, tile, outcomes, columns), lambda i: (site, 0, i, 0, 0))]
        + [ANY] * len(after),
        out_specs=pl.BlockSpec((outcomes, tile, columns), lambda i: (0, i, 0)),
        out_shape=jax.ShapeDtypeStruct((outcomes, rows, columns), stored_sites.dtype),
        compiler_params=params(),
        cost_estimate=cost(0, 8 * rows * outcomes * columns),
    )(stored_sites, *after)


def fetch(sources, code, view, target, sem):
    for at, ref in enumerate(sources):

        @pl.when(code == at)
        def _(ref=ref):
            pltpu.make_async_copy(view(ref), target, sem).start()


def gather(block, bond):
    return [block] + [
        lax.ppermute(block, "bond", [(i, (i + d) % bond) for i in range(bond)])
        for d in range(1, bond)
    ]


def pick(blocks, places, start, rows, after=()):
    count = places.shape[0]
    columns = blocks[0].shape[1]
    scalars = jnp.concatenate([places, jnp.reshape(start, (1,)).astype(jnp.int32)])

    def kernel(scalars_ref, *refs):
        sources = refs[: len(blocks)]
        target, sems = refs[-2:]
        begin = pl.multiple_of(scalars_ref[count], 16)

        def view(ref):
            return ref.at[pl.ds(begin, rows)]

        for slot in range(count):
            fetch(sources, scalars_ref[slot], view, target.at[slot], sems.at[slot])
        for slot in range(count):
            pltpu.make_async_copy(view(sources[0]), target.at[slot], sems.at[slot]).wait()

    return pl.pallas_call(
        kernel,
        grid_spec=pltpu.PrefetchScalarGridSpec(
            num_scalar_prefetch=1,
            grid=(1,),
            in_specs=[ANY] * (len(blocks) + len(after)),
            out_specs=pl.BlockSpec((count, rows, columns), lambda i, s: (0, 0, 0)),
            scratch_shapes=[pltpu.SemaphoreType.DMA((count,))],
        ),
        out_shape=jax.ShapeDtypeStruct((count, rows, columns), blocks[0].dtype),
        compiler_params=params(),
        cost_estimate=cost(0, 4 * count * rows * columns),
    )(scalars, *blocks, *after)


def partials(blocks, places, other, slabs, after=()):
    count = len(slabs)
    rows, depth = blocks[0].shape
    outcomes, _, columns = slabs[0].shape
    runs = len(other)
    part = rows // runs

    def kernel(places_ref, *refs):
        mine, refs = refs[: len(blocks)], refs[len(blocks) :]
        theirs, refs = refs[:runs], refs[runs:]
        weights, refs = refs[:count], refs[count:]
        own_out, other_out, left, sems = refs[-4:]

        @pl.when(pl.program_id(0) == 0)
        def _():
            def whole(ref):
                return ref

            def upper(slot):
                return left.at[slot, pl.ds(rows, rows)]

            def lower(run):
                return left.at[:, pl.ds(run * part, part)]

            for slot in range(count):
                fetch(mine, places_ref[slot], whole, upper(slot), sems.at[0, slot])
            for run in range(runs):
                fetch(theirs, places_ref[count + run], whole, lower(run), sems.at[1, run])
            for slot in range(count):
                pltpu.make_async_copy(mine[0], upper(slot), sems.at[0, slot]).wait()
            for run in range(runs):
                pltpu.make_async_copy(theirs[0], lower(run), sems.at[1, run]).wait()

        total = jnp.dot(left[0], weights[0][0], preferred_element_type=jnp.float32)
        for slot in range(1, count):
            total += jnp.dot(left[slot], weights[slot][0], preferred_element_type=jnp.float32)
        other_out[0] = total[:rows].astype(other_out.dtype)
        own_out[0] = total[rows:]

    result = pl.BlockSpec((1, rows, columns), lambda n, s: (n, 0, 0))
    size = outcomes * columns
    return pl.pallas_call(
        kernel,
        grid_spec=pltpu.PrefetchScalarGridSpec(
            num_scalar_prefetch=1,
            grid=(outcomes,),
            in_specs=[ANY] * (len(blocks) + runs)
            + [pl.BlockSpec((1, depth, columns), lambda n, s: (n, 0, 0))] * count
            + [ANY] * len(after),
            out_specs=[result, result],
            scratch_shapes=[
                pltpu.VMEM((count, 2 * rows, depth), blocks[0].dtype),
                pltpu.SemaphoreType.DMA((2, max(count, runs))),
            ],
        ),
        out_shape=[
            jax.ShapeDtypeStruct((outcomes, rows, columns), jnp.float32),
            jax.ShapeDtypeStruct((outcomes, rows, columns), jnp.bfloat16),
        ],
        compiler_params=params(),
        cost_estimate=cost(
            8 * count * rows * depth * size, 2 * count * depth * size + 6 * rows * size
        ),
    )(places, *blocks, *other, *slabs, *after)


def combine(own, received, chosen, kept, after=()):
    outcomes, rows, columns = own.shape
    tile = divisor(rows, 128)

    def kernel(own_ref, received_ref, chosen_ref, *refs):
        selected_ref, totals_ref = refs[-2:]
        picked = chosen_ref[...]
        lanes = lax.broadcasted_iota(jnp.int32, (tile, 128), 1)
        selected = jnp.zeros((tile, columns), jnp.float32)
        squares = jnp.zeros((tile, 128), jnp.float32)
        for n in range(outcomes):
            product = own_ref[n] + received_ref[n].astype(jnp.float32)
            selected = jnp.where(picked == n, product, selected)
            norm = jnp.sum(product * product, axis=1, keepdims=True)
            squares = jnp.where(lanes == n, norm, squares)
        selected_ref[...] = selected.astype(selected_ref.dtype)
        totals_ref[...] = squares.T[:8]

    block = pl.BlockSpec((outcomes, tile, columns), lambda i: (0, i, 0))
    selected, totals = pl.pallas_call(
        kernel,
        grid=(rows // tile,),
        in_specs=[block, block, pl.BlockSpec((tile, 1), lambda i: (i, 0))] + [ANY] * len(after),
        out_specs=[
            pl.BlockSpec((tile, columns), lambda i: (i, 0)),
            pl.BlockSpec((8, tile), lambda i: (0, i)),
        ],
        out_shape=[
            jax.ShapeDtypeStruct((rows, columns), kept),
            jax.ShapeDtypeStruct((8, rows), jnp.float32),
        ],
        compiler_params=params(),
        cost_estimate=cost(4 * outcomes * rows * columns, 8 * outcomes * rows * columns),
    )(own, received, chosen, *after)
    return selected, totals[:outcomes]


def body(env_start, stored_sites, slab_order, chosen, *, samp, bond):
    steps = stored_sites.shape[0]
    samples, width = env_start.shape
    inner = samp // 2
    mine = lax.axis_index("samp")
    half, place = mine // inner, mine % inner
    across = [(i, (i + inner) % samp) for i in range(samp)]
    column = lax.axis_index("bond")
    beside = [(i, i ^ 1) for i in range(bond)]

    def share(block):
        return [block] + [
            lax.ppermute(
                block,
                "samp",
                [(h * inner + i, h * inner + (i + d) % inner) for h in range(2) for i in range(inner)],
            )
            for d in range(1, inner)
        ]

    def places_of(site, which):
        ids = jnp.stack(
            [slab_order[site, which * inner + (place - d) % inner] for d in range(inner)]
        )
        return ((column - ids) % bond).astype(jnp.int32)

    side = column % 2
    runs = jnp.stack([side, 1 - side]).astype(jnp.int32)
    own_places = [jnp.concatenate([places_of(k, half), runs]) for k in range(steps)]
    other_places = [places_of(k, 1 - half) for k in range(steps)]

    chunks = CHUNKS
    rows = samples // chunks
    count = steps * chunks
    slabs = {0: share(outcome_major(stored_sites, 0))}
    env = {j: env_start[j * rows : (j + 1) * rows] for j in range(chunks)}
    blocks, halves, parts, received, outs = {}, {}, {}, {}, {}
    order = []

    def latest():
        return order[-1:]

    def start_gather(j):
        if 0 <= j < count:
            source = env[j] if j < chunks else outs[j - chunks][0]
            if j < chunks and order:
                source, _ = lax.optimization_barrier((source, order[-1]))
            blocks[j] = gather(source, bond)

    def start_cross(j):
        if 0 <= j < count:
            part = rows // 2
            sent = pick(blocks[j], other_places[j // chunks], side * part, part, latest())
            order.append(sent)
            halves[j] = [lax.ppermute(sent, "samp", across)]

    def start_swap(j):
        if 0 <= j < count:
            halves[j].append(lax.ppermute(halves[j][0], "bond", beside))

    def multiply(j):
        if 0 <= j < count:
            parts[j], sent = partials(
                blocks[j], own_places[j // chunks], halves[j], slabs[j // chunks], latest()
            )
            order.append(sent)
            received[j] = lax.ppermute(sent, "samp", across)

    def finish(j):
        if 0 <= j < count:
            site, c = j // chunks, j % chunks
            outs[j] = combine(
                parts[j],
                received[j],
                chosen[c * rows : (c + 1) * rows, site : site + 1],
                jnp.float32 if site + 1 == steps else jnp.bfloat16,
                latest(),
            )
            order.append(outs[j][0])

    def relay(k):
        if k < steps:
            slabs[k] = share(outcome_major(stored_sites, k, latest()))
            order.append(slabs[k][0])

    start_gather(0)
    start_cross(0)
    start_gather(1)
    start_swap(0)
    multiply(0)
    start_cross(1)
    start_gather(2)
    start_swap(1)
    start_cross(2)
    start_gather(3)
    for tick in range(1, count + 1):
        if tick > 1:
            finish(tick - 2)
            start_gather(tick + 2)
            start_cross(tick + 1)
        multiply(tick)
        relay(tick)
        start_swap(tick + 1)
    finish(count - 1)

    env = [outs[(steps - 1) * chunks + c][0] for c in range(chunks)]
    stacked = jnp.stack(
        [
            jnp.concatenate([outs[k * chunks + c][1] for c in range(chunks)], axis=1)
            for k in range(steps)
        ]
    )
    summed = stacked
    for d in range(1, bond):
        summed = summed + lax.ppermute(stacked, "bond", [(i, (i + d) % bond) for i in range(bond)])
    outcomes = jnp.arange(stored_sites.shape[3], dtype=jnp.int32)
    factor = jnp.ones((1, samples), jnp.float32)
    probabilities = []
    for site in range(steps):
        scaled = summed[site] * (factor * factor)
        probabilities.append(scaled / jnp.sum(scaled, axis=0, keepdims=True))
        selector = chosen[:, site][None, :] == outcomes[:, None]
        chosen_total = jnp.sum(jnp.where(selector, scaled, 0.0), axis=0, keepdims=True)
        factor = factor * lax.rsqrt(chosen_total / (width * bond) + epsilon)
    env_final = jnp.concatenate(env, axis=0) * factor[0][:, None]
    return jnp.stack(probabilities).transpose(2, 0, 1), env_final


def plain_body(env_start, stored_sites, slab_order, chosen):
    samples = env_start.shape[0]
    steps = stored_sites.shape[0]
    slab = stored_sites.shape[2]
    outcomes = jnp.arange(stored_sites.shape[3], dtype=jnp.int32)
    gathered = lax.all_gather(env_start, "bond", axis=1, tiled=True)
    bond_width = gathered.shape[1]
    factor = jnp.ones((samples,), jnp.float32)
    prob_list, raw_totals, selectors = [], [], []
    selected = None
    for site in range(steps):
        ordered = jnp.concatenate(
            [
                lax.dynamic_slice_in_dim(gathered, slab_order[site, i] * slab, slab, axis=1)
                for i in range(slab_order.shape[1])
            ],
            axis=1,
        )
        portion = lax.all_gather(stored_sites[site], "samp", axis=0, tiled=True)
        product = jnp.dot(
            ordered, portion.reshape(bond_width, -1), preferred_element_type=jnp.float32
        )
        product = lax.optimization_barrier(product)
        product = product.reshape(samples, stored_sites.shape[3], stored_sites.shape[4])
        selector = (chosen[:, site][:, None] == outcomes[None, :]).astype(jnp.float32)
        selected = jnp.sum(selector[:, :, None] * product, axis=1)
        raw_totals.append(jnp.sum(product * product, axis=2))
        selectors.append(selector)
        if site + 1 < steps:
            gathered = lax.all_gather(selected.astype(jnp.bfloat16), "bond", axis=1, tiled=True)
    reduced = lax.psum(tuple(raw_totals), "bond")
    for site in range(steps):
        totals = reduced[site] * (factor * factor)[:, None]
        prob_list.append(totals / jnp.sum(totals, axis=1, keepdims=True))
        chosen_total = jnp.sum(totals * selectors[site], axis=1)
        factor = factor * lax.rsqrt(chosen_total / bond_width + epsilon)
    return jnp.stack(prob_list, axis=1), selected * factor[:, None]


def solution(mesh):
    samp, bond = mesh.shape["samp"], mesh.shape["bond"]

    def choose(env_start, stored_sites, slab_order, chosen):
        if stored_sites.shape[2] == env_start.shape[1] and samp == 4 and bond == 4:
            return body(env_start, stored_sites, slab_order, chosen, samp=samp, bond=bond)
        return plain_body(env_start, stored_sites, slab_order, chosen)

    return jax.shard_map(
        choose,
        mesh=mesh,
        in_specs=(
            P(("parts", "samp"), "bond"),
            P("parts", "samp", None, None, "bond"),
            P("parts", None),
            P(("parts", "samp"), None),
        ),
        out_specs=(P(("parts", "samp"), None, None), P(("parts", "samp"), "bond")),
        check_vma=False,
    )
```

time: 411 us -> 345 us (0.84)
  waiting for transfers between devices: 152 us -> 101 us
  starting transfers between devices: 108 us -> 77.9 us
  local copies, waits for them, and re-layouts: 17.2 us -> 36.3 us
    ppermute x42 -> x50, waiting for transfers between devices: 148 us -> 98.9 us  [the longest x8 43.2 us: multiply(): received[j] = lax.ppermute(sent, 'samp', across)]
    ppermute x42 -> x50, starting transfers between devices: 105 us -> 73.2 us  [the longest x24 37.1 us: gather(): lax.ppermute(block, 'bond', [(i, (i + d) % bond) for i in range(bond)])]
    unnamed x46 -> x188, local copies, waits for them, and re-layouts: 16.2 us -> 34.1 us
    pallas_call x8, Pallas kernels: 12.7 us -> 6.04 us  [combine(): pl.pallas_call(kernel, grid=(rows // tile,), in_specs=[block, block, pl.B...]
  transfers between devices with their start and end apart: 45 -> 53, of which waited for: 19 -> 20; matrix products, arithmetic and copies ran while one was open for 2% -> 3% of each run, Pallas kernels for 27% -> 31%
where the time goes in v2:
time: 345 us; the launch traced here: 343 us
  Pallas kernels  119 us (34%)
  waiting for transfers between devices  101 us (29%)
  starting transfers between devices  77.9 us (23%)
  local copies, waits for them, and re-layouts  36.3 us (11%)
  other arithmetic  7.75 us (2%)
    pallas_call x8, Pallas kernels, partials(): pl.pallas_call(kernel, grid_spec=pltpu.PrefetchScalarGridSpec(num_scalar_...  83.7 us
    ppermute x8, waiting for transfers between devices, multiply(): received[j] = lax.ppermute(sent, 'samp', across)  43.2 us
    ppermute x24, starting transfers between devices, gather(): lax.ppermute(block, 'bond', [(i, (i + d) % bond) for i in range(bond)])  37.1 us
    unnamed x188, local copies, waits for them, and re-layouts  34.1 us
    ppermute x24, waiting for transfers between devices, gather(): lax.ppermute(block, 'bond', [(i, (i + d) % bond) for i in range(bond)])  24.9 us
    pallas_call x2, Pallas kernels, outcome_major(): pl.pallas_call(kernel, grid=(rows // tile,), in_specs=[pl.BlockSpec((1, 1...  19.5 us
    ppermute x8, waiting for transfers between devices, start_swap(): halves[j].append(lax.ppermute(halves[j][0], 'bond', beside))  17.5 us
    ppermute x8, starting transfers between devices, start_swap(): halves[j].append(lax.ppermute(halves[j][0], 'bond', beside))  16.4 us
  transfers between devices with their start and end apart: 53, of which 20 were waited for; matrix products, arithmetic and copies ran while one was open for 3% of the time, Pallas kernels for 31%

profile of v2, /device:TPU:0, one launch (start us, length us, event | category | flops | bytes accessed | tf_op | source)
XLA Modules:
  0.0 343.4 jit_solution(709495956000183411)
XLA Ops:
  0.6 9.8 %shard_map.60.refs_6_ = bf16[4,1024,1024]{2,1,0:T(8,128)(2,1)} custom-call(bf16[2,1,1024,4,1024]{4,3,2,1,0:T(4,128)(2,1)} %source.3), custom_call_target="tpu_custom_call" | custom-call | bytes 335544320 | tf_op jit(solution)/shard_map/pallas_call | solution.py:43
  11.8 2.6 collective-permute-start
  14.3 2.6 collective-permute-start.1
  20.3 3.3 collective-permute-done.refs_1_
  23.7 11.0 %collective-permute-done.1.refs_2_ = bf16[128,1024]{1,0:T(8,128)(2,1)S(1)} collective-permute-done((bf16[128,1024]{1,0:T(8,128)(2,1)S(1)}, bf16[128,1024]{1,0:T(8,128)(2,1)S(1)}, u32[]{:S(2)}, u32[]{:S(2)}) %collective-permute-start.1) | collective-permute-done | bytes 262176 | tf_op jit(solution)/shard_map/ppermute | solution.py:65
  37.9 6.0 %collective-permute-done.3.refs_4_ = bf16[2,64,1024]{2,1,0:T(8,128)(2,1)S(1)} collective-permute-done((bf16[2,64,1024]{2,1,0:T(8,128)(2,1)S(1)}, bf16[2,64,1024]{2,1,0:T(8,128)(2,1)S(1)}, u32[]{:S(2)}, u32[]{:S(2)}) %collective-permute-start.3) | collective-permute-done | bytes 262176 | tf_op jit(solution)/shard_map/ppermute | solution.py:260
  43.9 6.2 %collective-permute-start.4 = (bf16[2,64,1024]{2,1,0:T(8,128)(2,1)S(1)}, bf16[2,64,1024]{2,1,0:T(8,128)(2,1)S(1)}, u32[]{:S(2)}, u32[]{:S(2)}) collective-permute-start(bf16[2,64,1024]{2,1,0:T(8,128)(2,1)S(1)} %collective-permute-done.3.refs_4_), channel_id=1, source_target_pairs={{0,1},{1,0},{2,3},{3,2},{4,5},{5,4},{6,7},{7,6},{8,9},{9,8},{10,11... | collective-permute-start | bytes 786440 | tf_op jit(solution)/shard_map/ppermute | solution.py:264
  53.4 2.9 collective-permute-start.9
  56.3 7.5 %collective-permute-done.4.refs_5_ = bf16[2,64,1024]{2,1,0:T(8,128)(2,1)S(1)} collective-permute-done((bf16[2,64,1024]{2,1,0:T(8,128)(2,1)S(1)}, bf16[2,64,1024]{2,1,0:T(8,128)(2,1)S(1)}, u32[]{:S(2)}, u32[]{:S(2)}) %collective-permute-start.4) | collective-permute-done | bytes 262176 | tf_op jit(solution)/shard_map/ppermute | solution.py:264
  71.1 9.2 %shard_map.61 = (f32[4,128,1024]{2,1,0:T(8,128)S(1)}, bf16[4,128,1024]{2,1,0:T(8,128)(2,1)S(1)}) custom-call(s32[4]{0:T(128)S(1)} %add_add_fusion.1.places_ref, bf16[128,1024]{1,0:T(8,128)(2,1)S(1)} %copy-done.7, bf16[128,1024]{1,0:T(8,128)(2,1)S(1)} %copy-done.19, bf16[128,1024]{1,0:T(8,128)(2,1)S(1)} %copy-done.21, bf16[128,1024]{1,0:T(8,128)(2,1)S(1)} %copy-done.23, ...), custom_call_target="tpu_custom_call" | custom-call | flops 85899345920 | bytes 199229440 | tf_op jit(solution)/shard_map/pallas_call | solution.py:144
  81.5 3.7 %collective-permute-start.14 = (bf16[128,1024]{1,0:T(8,128)(2,1)S(1)}, bf16[128,1024]{1,0:T(8,128)(2,1)S(1)}, u32[]{:S(2)}, u32[]{:S(2)}) collective-permute-start(bf16[128,1024]{1,0:T(8,128)(2,1)S(1)} %copy-done.14), channel_id=1, source_target_pairs={{0,3},{1,0},{2,1},{3,2},{4,7},{5,4},{6,5},{7,6},{8,11},{9,8},{10,9... | collective-permute-start | bytes 786440 | tf_op jit(solution)/shard_map/ppermute | solution.py:65
  86.7 3.1 collective-permute-done.12.refs_1_
  89.8 7.5 %collective-permute-done.13.refs_2_ = bf16[128,1024]{1,0:T(8,128)(2,1)S(1)} collective-permute-done((bf16[128,1024]{1,0:T(8,128)(2,1)S(1)}, bf16[128,1024]{1,0:T(8,128)(2,1)S(1)}, u32[]{:S(2)}, u32[]{:S(2)}) %collective-permute-start.13) | collective-permute-done | bytes 262176 | tf_op jit(solution)/shard_map/ppermute | solution.py:65
  100.5 3.4 collective-permute-start.11
  106.6 3.0 collective-permute-start.19
  109.6 10.0 %collective-permute-done.11.refs_5_ = bf16[2,64,1024]{2,1,0:T(8,128)(2,1)} collective-permute-done((bf16[2,64,1024]{2,1,0:T(8,128)(2,1)}, bf16[2,64,1024]{2,1,0:T(8,128)(2,1)}, u32[]{:S(2)}, u32[]{:S(2)}) %collective-permute-start.11) | collective-permute-done | bytes 262176 | tf_op jit(solution)/shard_map/ppermute | solution.py:264
  119.7 2.0 collective-permute-start.17
  124.5 10.5 %shard_map.64 = (f32[4,128,1024]{2,1,0:T(8,128)S(1)}, bf16[4,128,1024]{2,1,0:T(8,128)(2,1)S(1)}) custom-call(s32[4]{0:T(128)S(1)} %add_add_fusion.1.places_ref, bf16[128,1024]{1,0:T(8,128)(2,1)S(1)} %get-tuple-element.39.refs_0_, bf16[128,1024]{1,0:T(8,128)(2,1)S(1)} %copy-done.25, bf16[128,1024]{1,0:T(8,128)(2,1)S(1)} %copy-done.27, ...), custom_call_target="tpu_custom_call" | custom-call | flops 85899345920 | bytes 199229440 | tf_op jit(solution)/shard_map/pallas_call | solution.py:144
  135.1 9.7 %shard_map.65.refs_0_.refs_6_ = bf16[4,1024,1024]{2,1,0:T(8,128)(2,1)} custom-call(bf16[2,1,1024,4,1024]{4,3,2,1,0:T(4,128)(2,1)} %source.3, bf16[4,128,1024]{2,1,0:T(8,128)(2,1)S(1)} %get-tuple-element.41.refs_0_), custom_call_target="tpu_custom_call" | custom-call | bytes 335544320 | tf_op jit(solution)/shard_map/pallas_call | solution.py:43
  146.0 3.4 collective-permute-start.26
  150.4 2.1 collective-permute-start.22
  152.4 11.3 %shard_map.68 = (f32[4,128,1024]{2,1,0:T(8,128)S(1)}, bf16[4,128,1024]{2,1,0:T(8,128)(2,1)}) custom-call(s32[4]{0:T(128)S(1)} %add_add_fusion.1.places_ref, bf16[128,1024]{1,0:T(8,128)(2,1)S(1)} %copy-done.15, bf16[128,1024]{1,0:T(8,128)(2,1)S(1)} %copy-done.51, bf16[128,1024]{1,0:T(8,128)(2,1)S(1)} %copy-done.55, bf16[128,1024]{1,0:T(8,128)(2,1)S(1)} %copy-done.57, ...), custom_call_target="tpu_custom_call" | custom-call | flops 85899345920 | bytes 199229440 | tf_op jit(solution)/shard_map/pallas_call | solution.py:144
  170.7 1.7 collective-permute-start.31
  173.1 1.8 collective-permute-start.32
  175.5 3.6 %collective-permute-start.33 = (bf16[128,1024]{1,0:T(8,128)(2,1)}, bf16[128,1024]{1,0:T(8,128)(2,1)S(1)}, u32[]{:S(2)}, u32[]{:S(2)}) collective-permute-start(bf16[128,1024]{1,0:T(8,128)(2,1)} %get-tuple-element.49.refs_4_.refs_0_), channel_id=1, source_target_pairs={{0,3},{1,0},{2,1},{3,2},{4,7},{5,4},{6,5},{7,6},{8,11},{9,8},{10,9... | collective-permute-start | bytes 786440 | tf_op jit(solution)/shard_map/ppermute | solution.py:65
  185.8 9.2 %shard_map.71 = (f32[4,128,1024]{2,1,0:T(8,128)S(1)}, bf16[4,128,1024]{2,1,0:T(8,128)(2,1)S(1)}) custom-call(s32[4]{0:T(128)S(1)} %add_add_fusion.1.places_ref, bf16[128,1024]{1,0:T(8,128)(2,1)S(1)} %copy-done.13, bf16[128,1024]{1,0:T(8,128)(2,1)S(1)} %copy-done.41, bf16[128,1024]{1,0:T(8,128)(2,1)S(1)} %copy-done.45, bf16[128,1024]{1,0:T(8,128)(2,1)S(1)} %copy-done.49, ...), custom_call_target="tpu_custom_call" | custom-call | flops 85899345920 | bytes 199229440 | tf_op jit(solution)/shard_map/pallas_call | solution.py:144
  195.0 1.7 collective-permute-done.21.received_ref
  196.6 1.7 collective-permute-start.29
  209.5 1.9 collective-permute-start.39
  214.7 10.5 %shard_map.74 = (f32[4,128,1024]{2,1,0:T(8,128)S(1)}, bf16[4,128,1024]{2,1,0:T(8,128)(2,1)S(1)}) custom-call(s32[4]{0:T(128)S(1)} %add_add_fusion.2.places_ref, bf16[128,1024]{1,0:T(8,128)(2,1)S(1)} %get-tuple-element.45.refs_4_.refs_0_, bf16[128,1024]{1,0:T(8,128)(2,1)S(1)} %copy-done.33, bf16[128,1024]{1,0:T(8,128)(2,1)S(1)} %copy-done.35, ...), custom_call_target="tpu_custom_call" | custom-call | flops 85899345920 | bytes 199229440 | tf_op jit(solution)/shard_map/pallas_call | solution.py:144
  225.3 5.2 %collective-permute-done.27.received_ref = bf16[4,128,1024]{2,1,0:T(8,128)(2,1)S(1)} collective-permute-done((bf16[4,128,1024]{2,1,0:T(8,128)(2,1)S(1)}, bf16[4,128,1024]{2,1,0:T(8,128)(2,1)S(1)}, u32[]{:S(2)}, u32[]{:S(2)}) %collective-permute-start.27) | collective-permute-done | bytes 1048608 | tf_op jit(solution)/shard_map/ppermute | solution.py:272
  230.5 1.7 collective-permute-start.34
  233.4 1.7 collective-permute-start.44
  235.2 1.9 collective-permute-start.45
  239.3 10.5 %shard_map.77 = (f32[4,128,1024]{2,1,0:T(8,128)S(1)}, bf16[4,128,1024]{2,1,0:T(8,128)(2,1)S(1)}) custom-call(s32[4]{0:T(128)S(1)} %add_add_fusion.2.places_ref, bf16[128,1024]{1,0:T(8,128)(2,1)} %get-tuple-element.49.refs_4_.refs_0_, bf16[128,1024]{1,0:T(8,128)(2,1)S(1)} %copy-done.39, bf16[128,1024]{1,0:T(8,128)(2,1)S(1)} %copy-done.43, ...), custom_call_target="tpu_custom_call" | custom-call | flops 85899345920 | bytes 199229440 | tf_op jit(solution)/shard_map/pallas_call | solution.py:144
  249.8 6.8 %collective-permute-done.34.received_ref = bf16[4,128,1024]{2,1,0:T(8,128)(2,1)S(1)} collective-permute-done((bf16[4,128,1024]{2,1,0:T(8,128)(2,1)S(1)}, bf16[4,128,1024]{2,1,0:T(8,128)(2,1)S(1)}, u32[]{:S(2)}, u32[]{:S(2)}) %collective-permute-start.34) | collective-permute-done | bytes 1048608 | tf_op jit(solution)/shard_map/ppermute | solution.py:272
  259.6 1.7 collective-permute-start.47
  262.1 1.8 collective-permute-start.40
  263.8 5.0 %collective-permute-done.47.refs_4_ = bf16[2,64,1024]{2,1,0:T(8,128)(2,1)} collective-permute-done((bf16[2,64,1024]{2,1,0:T(8,128)(2,1)}, bf16[2,64,1024]{2,1,0:T(8,128)(2,1)}, u32[]{:S(2)}, u32[]{:S(2)}) %collective-permute-start.47) | collective-permute-done | bytes 262176 | tf_op jit(solution)/shard_map/ppermute | solution.py:260
  268.8 2.3 collective-permute-start.48
  274.0 11.3 %shard_map.80 = (f32[4,128,1024]{2,1,0:T(8,128)S(1)}, bf16[4,128,1024]{2,1,0:T(8,128)(2,1)}) custom-call(s32[4]{0:T(128)S(1)} %copy-done.73, bf16[128,1024]{1,0:T(8,128)(2,1)S(1)} %copy-done.9, bf16[128,1024]{1,0:T(8,128)(2,1)S(1)} %copy-done.53, bf16[128,1024]{1,0:T(8,128)(2,1)S(1)} %copy-done.59, bf16[128,1024]{1,0:T(8,128)(2,1)S(1)} %copy-done.61, ...), custom_call_target="tpu_custom_call" | custom-call | flops 85899345920 | bytes 199229440 | tf_op jit(solution)/shard_map/pallas_call | solution.py:144
  287.0 4.2 %collective-permute-done.40.received_ref = bf16[4,128,1024]{2,1,0:T(8,128)(2,1)S(1)} collective-permute-done((bf16[4,128,1024]{2,1,0:T(8,128)(2,1)S(1)}, bf16[4,128,1024]{2,1,0:T(8,128)(2,1)S(1)}, u32[]{:S(2)}, u32[]{:S(2)}) %collective-permute-start.40) | collective-permute-done | bytes 1048608 | tf_op jit(solution)/shard_map/ppermute | solution.py:272
  292.4 11.3 %shard_map.82 = (f32[4,128,1024]{2,1,0:T(8,128)S(1)}, bf16[4,128,1024]{2,1,0:T(8,128)(2,1)}) custom-call(s32[4]{0:T(128)S(1)} %copy-done.73, bf16[128,1024]{1,0:T(8,128)(2,1)S(1)} %copy-done.11, bf16[128,1024]{1,0:T(8,128)(2,1)S(1)} %copy-done.63, bf16[128,1024]{1,0:T(8,128)(2,1)S(1)} %copy-done.65, bf16[128,1024]{1,0:T(8,128)(2,1)S(1)} %copy-done.67, ...), custom_call_target="tpu_custom_call" | custom-call | flops 85899345920 | bytes 199229440 | tf_op jit(solution)/shard_map/pallas_call | solution.py:144
  304.9 8.8 %collective-permute-done.46.received_ref = bf16[4,128,1024]{2,1,0:T(8,128)(2,1)} collective-permute-done((bf16[4,128,1024]{2,1,0:T(8,128)(2,1)}, bf16[4,128,1024]{2,1,0:T(8,128)(2,1)}, u32[]{:S(2)}, u32[]{:S(2)}) %collective-permute-start.46) | collective-permute-done | bytes 1048608 | tf_op jit(solution)/shard_map/ppermute | solution.py:272
  315.3 1.7 shard_map.83
  317.1 16.5 %collective-permute-done.49.received_ref = bf16[4,128,1024]{2,1,0:T(8,128)(2,1)S(1)} collective-permute-done((bf16[4,128,1024]{2,1,0:T(8,128)(2,1)}, bf16[4,128,1024]{2,1,0:T(8,128)(2,1)S(1)}, u32[]{:S(2)}, u32[]{:S(2)}) %collective-permute-start.49) | collective-permute-done | bytes 1048608 | tf_op jit(solution)/shard_map/ppermute | solution.py:272
  334.2 2.3 collective-permute-start.50
  336.5 2.4 collective-permute-start.52
  (303 shorter events, 82.1 us)
Async XLA Ops:
  10.4 54.0 %collective-permute-start.5 = (bf16[4,1024,1024]{2,1,0:T(8,128)(2,1)}, bf16[4,1024,1024]{2,1,0:T(8,128)(2,1)}, u32[]{:S(2)}, u32[]{:S(2)}) collective-permute-start(bf16[4,1024,1024]{2,1,0:T(8,128)(2,1)} %shard_map.60.refs_6_), channel_id=1, source_target_pairs={{0,4},{4,0},{8,12},{12,8},{1,5},{5,1},{9,13},{13,9},{2,6},{6,2},{1... | collective-permute-start | bytes 25165832 | tf_op jit(solution)/shard_map/ppermute | solution.py:218
  11.8 11.9 %collective-permute-start = (bf16[128,1024]{1,0:T(8,128)(2,1)S(1)}, bf16[128,1024]{1,0:T(8,128)(2,1)S(1)}, u32[]{:S(2)}, u32[]{:S(2)}) collective-permute-start(bf16[128,1024]{1,0:T(8,128)(2,1)S(1)} %get-tuple-element.74.refs_0_), channel_id=1, source_target_pairs={{0,1},{1,2},{2,3},{3,0},{4,5},{5,6},{6,7},{7,4},{8,9},{9,10},{10,1... | collective-permute-start | bytes 786440 | tf_op jit(solution)/shard_map/ppermute | solution.py:65
  14.3 20.3 %collective-permute-start.1 = (bf16[128,1024]{1,0:T(8,128)(2,1)S(1)}, bf16[128,1024]{1,0:T(8,128)(2,1)S(1)}, u32[]{:S(2)}, u32[]{:S(2)}) collective-permute-start(bf16[128,1024]{1,0:T(8,128)(2,1)S(1)} %get-tuple-element.74.refs_0_), channel_id=1, source_target_pairs={{0,2},{1,3},{2,0},{3,1},{4,6},{5,7},{6,4},{7,5},{8,10},{9,11},{10,... | collective-permute-start | bytes 786440 | tf_op jit(solution)/shard_map/ppermute | solution.py:65
  16.9 17.8 %collective-permute-start.2 = (bf16[128,1024]{1,0:T(8,128)(2,1)S(1)}, bf16[128,1024]{1,0:T(8,128)(2,1)S(1)}, u32[]{:S(2)}, u32[]{:S(2)}) collective-permute-start(bf16[128,1024]{1,0:T(8,128)(2,1)S(1)} %get-tuple-element.74.refs_0_), channel_id=1, source_target_pairs={{0,3},{1,0},{2,1},{3,2},{4,7},{5,4},{6,5},{7,6},{8,11},{9,8},{10,9... | collective-permute-start | bytes 786440 | tf_op jit(solution)/shard_map/ppermute | solution.py:65
  35.6 8.3 %collective-permute-start.3 = (bf16[2,64,1024]{2,1,0:T(8,128)(2,1)S(1)}, bf16[2,64,1024]{2,1,0:T(8,128)(2,1)S(1)}, u32[]{:S(2)}, u32[]{:S(2)}) collective-permute-start(bf16[2,64,1024]{2,1,0:T(8,128)(2,1)S(1)} %shard_map.59.refs_8_), channel_id=1, source_target_pairs={{0,8},{4,12},{8,0},{12,4},{1,9},{5,13},{9,1},{13,5},{2,10},{6,14},... | collective-permute-start | bytes 786440 | tf_op jit(solution)/shard_map/ppermute | solution.py:260
  43.9 19.9 %collective-permute-start.4 = (bf16[2,64,1024]{2,1,0:T(8,128)(2,1)S(1)}, bf16[2,64,1024]{2,1,0:T(8,128)(2,1)S(1)}, u32[]{:S(2)}, u32[]{:S(2)}) collective-permute-start(bf16[2,64,1024]{2,1,0:T(8,128)(2,1)S(1)} %collective-permute-done.3.refs_4_), channel_id=1, source_target_pairs={{0,1},{1,0},{2,3},{3,2},{4,5},{5,4},{6,7},{7,6},{8,9},{9,8},{10,11... | collective-permute-start | bytes 786440 | tf_op jit(solution)/shard_map/ppermute | solution.py:264
  52.1 28.2 %collective-permute-start.7 = (bf16[128,1024]{1,0:T(8,128)(2,1)S(1)}, bf16[128,1024]{1,0:T(8,128)(2,1)S(1)}, u32[]{:S(2)}, u32[]{:S(2)}) collective-permute-start(bf16[128,1024]{1,0:T(8,128)(2,1)S(1)} %get-tuple-element.39.refs_0_), channel_id=1, source_target_pairs={{0,1},{1,2},{2,3},{3,0},{4,5},{5,6},{6,7},{7,4},{8,9},{9,10},{10,1... | collective-permute-start | bytes 786440 | tf_op jit(solution)/shard_map/ppermute | solution.py:65
  52.1 28.2 %collective-permute-start.8 = (bf16[128,1024]{1,0:T(8,128)(2,1)S(1)}, bf16[128,1024]{1,0:T(8,128)(2,1)S(1)}, u32[]{:S(2)}, u32[]{:S(2)}) collective-permute-start(bf16[128,1024]{1,0:T(8,128)(2,1)S(1)} %get-tuple-element.39.refs_0_), channel_id=1, source_target_pairs={{0,2},{1,3},{2,0},{3,1},{4,6},{5,7},{6,4},{7,5},{8,10},{9,11},{10,... | collective-permute-start | bytes 786440 | tf_op jit(solution)/shard_map/ppermute | solution.py:65
  53.4 26.9 %collective-permute-start.9 = (bf16[128,1024]{1,0:T(8,128)(2,1)S(1)}, bf16[128,1024]{1,0:T(8,128)(2,1)S(1)}, u32[]{:S(2)}, u32[]{:S(2)}) collective-permute-start(bf16[128,1024]{1,0:T(8,128)(2,1)S(1)} %get-tuple-element.39.refs_0_), channel_id=1, source_target_pairs={{0,3},{1,0},{2,1},{3,2},{4,7},{5,4},{6,5},{7,6},{8,11},{9,8},{10,9... | collective-permute-start | bytes 786440 | tf_op jit(solution)/shard_map/ppermute | solution.py:65
  81.3 8.4 %collective-permute-start.12 = (bf16[128,1024]{1,0:T(8,128)(2,1)S(1)}, bf16[128,1024]{1,0:T(8,128)(2,1)S(1)}, u32[]{:S(2)}, u32[]{:S(2)}) collective-permute-start(bf16[128,1024]{1,0:T(8,128)(2,1)S(1)} %copy-done.14), channel_id=1, source_target_pairs={{0,1},{1,2},{2,3},{3,0},{4,5},{5,6},{6,7},{7,4},{8,9},{9,10},{10,1... | collective-permute-start | bytes 786440 | tf_op jit(solution)/shard_map/ppermute | solution.py:65
  81.5 15.7 %collective-permute-start.13 = (bf16[128,1024]{1,0:T(8,128)(2,1)S(1)}, bf16[128,1024]{1,0:T(8,128)(2,1)S(1)}, u32[]{:S(2)}, u32[]{:S(2)}) collective-permute-start(bf16[128,1024]{1,0:T(8,128)(2,1)S(1)} %copy-done.14), channel_id=1, source_target_pairs={{0,2},{1,3},{2,0},{3,1},{4,6},{5,7},{6,4},{7,5},{8,10},{9,11},{10,... | collective-permute-start | bytes 786440 | tf_op jit(solution)/shard_map/ppermute | solution.py:65
  81.5 15.7 %collective-permute-start.14 = (bf16[128,1024]{1,0:T(8,128)(2,1)S(1)}, bf16[128,1024]{1,0:T(8,128)(2,1)S(1)}, u32[]{:S(2)}, u32[]{:S(2)}) collective-permute-start(bf16[128,1024]{1,0:T(8,128)(2,1)S(1)} %copy-done.14), channel_id=1, source_target_pairs={{0,3},{1,0},{2,1},{3,2},{4,7},{5,4},{6,5},{7,6},{8,11},{9,8},{10,9... | collective-permute-start | bytes 786440 | tf_op jit(solution)/shard_map/ppermute | solution.py:65
  85.2 15.2 %collective-permute-start.10 = (bf16[2,64,1024]{2,1,0:T(8,128)(2,1)S(1)}, bf16[2,64,1024]{2,1,0:T(8,128)(2,1)}, u32[]{:S(2)}, u32[]{:S(2)}) collective-permute-start(bf16[2,64,1024]{2,1,0:T(8,128)(2,1)S(1)} %shard_map.62.refs_4_), channel_id=1, source_target_pairs={{0,8},{4,12},{8,0},{12,4},{1,9},{5,13},{9,1},{13,5},{2,10},{6,14},... | collective-permute-start | bytes 786440 | tf_op jit(solution)/shard_map/ppermute | solution.py:260
  98.9 20.8 %collective-permute-start.16 = (bf16[2,64,1024]{2,1,0:T(8,128)(2,1)}, bf16[2,64,1024]{2,1,0:T(8,128)(2,1)}, u32[]{:S(2)}, u32[]{:S(2)}) collective-permute-start(bf16[2,64,1024]{2,1,0:T(8,128)(2,1)} %shard_map.63.refs_8_), channel_id=1, source_target_pairs={{0,8},{4,12},{8,0},{12,4},{1,9},{5,13},{9,1},{13,5},{2,10},{6,14},... | collective-permute-start | bytes 786440 | tf_op jit(solution)/shard_map/ppermute | solution.py:260
  100.5 19.2 %collective-permute-start.11 = (bf16[2,64,1024]{2,1,0:T(8,128)(2,1)}, bf16[2,64,1024]{2,1,0:T(8,128)(2,1)}, u32[]{:S(2)}, u32[]{:S(2)}) collective-permute-start(bf16[2,64,1024]{2,1,0:T(8,128)(2,1)} %collective-permute-done.10.refs_4_), channel_id=1, source_target_pairs={{0,1},{1,0},{2,3},{3,2},{4,5},{5,4},{6,7},{7,6},{8,9},{9,8},{10,11... | collective-permute-start | bytes 786440 | tf_op jit(solution)/shard_map/ppermute | solution.py:264
  106.1 38.7 %collective-permute-start.6 = (bf16[4,128,1024]{2,1,0:T(8,128)(2,1)S(1)}, bf16[4,128,1024]{2,1,0:T(8,128)(2,1)S(1)}, u32[]{:S(2)}, u32[]{:S(2)}) collective-permute-start(bf16[4,128,1024]{2,1,0:T(8,128)(2,1)S(1)} %get-tuple-element.38.refs_4_), channel_id=1, source_target_pairs={{0,8},{4,12},{8,0},{12,4},{1,9},{5,13},{9,1},{13,5},{2,10},{6,14},... | collective-permute-start | bytes 3145736 | tf_op jit(solution)/shard_map/ppermute | solution.py:272
  106.6 38.7 %collective-permute-start.18 = (bf16[128,1024]{1,0:T(8,128)(2,1)}, bf16[128,1024]{1,0:T(8,128)(2,1)S(1)}, u32[]{:S(2)}, u32[]{:S(2)}) collective-permute-start(bf16[128,1024]{1,0:T(8,128)(2,1)} %get-tuple-element.44.refs_0_), channel_id=1, source_target_pairs={{0,1},{1,2},{2,3},{3,0},{4,5},{5,6},{6,7},{7,4},{8,9},{9,10},{10,1... | collective-permute-start | bytes 786440 | tf_op jit(solution)/shard_map/ppermute | solution.py:65
  106.6 38.8 %collective-permute-start.19 = (bf16[128,1024]{1,0:T(8,128)(2,1)}, bf16[128,1024]{1,0:T(8,128)(2,1)S(1)}, u32[]{:S(2)}, u32[]{:S(2)}) collective-permute-start(bf16[128,1024]{1,0:T(8,128)(2,1)} %get-tuple-element.44.refs_0_), channel_id=1, source_target_pairs={{0,2},{1,3},{2,0},{3,1},{4,6},{5,7},{6,4},{7,5},{8,10},{9,11},{10,... | collective-permute-start | bytes 786440 | tf_op jit(solution)/shard_map/ppermute | solution.py:65
  119.7 26.3 %collective-permute-start.20 = (bf16[128,1024]{1,0:T(8,128)(2,1)}, bf16[128,1024]{1,0:T(8,128)(2,1)S(1)}, u32[]{:S(2)}, u32[]{:S(2)}) collective-permute-start(bf16[128,1024]{1,0:T(8,128)(2,1)} %get-tuple-element.44.refs_0_), channel_id=1, source_target_pairs={{0,3},{1,0},{2,1},{3,2},{4,7},{5,4},{6,5},{7,6},{8,11},{9,8},{10,9... | collective-permute-start | bytes 786440 | tf_op jit(solution)/shard_map/ppermute | solution.py:65
  119.7 30.6 %collective-permute-start.17 = (bf16[2,64,1024]{2,1,0:T(8,128)(2,1)}, bf16[2,64,1024]{2,1,0:T(8,128)(2,1)S(1)}, u32[]{:S(2)}, u32[]{:S(2)}) collective-permute-start(bf16[2,64,1024]{2,1,0:T(8,128)(2,1)} %collective-permute-done.16.refs_4_), channel_id=1, source_target_pairs={{0,1},{1,0},{2,3},{3,2},{4,5},{5,4},{6,7},{7,6},{8,9},{9,8},{10,11... | collective-permute-start | bytes 786440 | tf_op jit(solution)/shard_map/ppermute | solution.py:264
  144.8 20.7 %collective-permute-start.15 = (bf16[4,128,1024]{2,1,0:T(8,128)(2,1)S(1)}, bf16[4,128,1024]{2,1,0:T(8,128)(2,1)S(1)}, u32[]{:S(2)}, u32[]{:S(2)}) collective-permute-start(bf16[4,128,1024]{2,1,0:T(8,128)(2,1)S(1)} %get-tuple-element.41.refs_0_), channel_id=1, source_target_pairs={{0,8},{4,12},{8,0},{12,4},{1,9},{5,13},{9,1},{13,5},{2,10},{6,14},... | collective-permute-start | bytes 3145736 | tf_op jit(solution)/shard_map/ppermute | solution.py:272
  145.4 21.3 %collective-permute-start.24 = (bf16[128,1024]{1,0:T(8,128)(2,1)S(1)}, bf16[128,1024]{1,0:T(8,128)(2,1)S(1)}, u32[]{:S(2)}, u32[]{:S(2)}) collective-permute-start(bf16[128,1024]{1,0:T(8,128)(2,1)S(1)} %get-tuple-element.45.refs_4_.refs_0_), channel_id=1, source_target_pairs={{0,1},{1,2},{2,3},{3,0},{4,5},{5,6},{6,7},{7,4},{8,9},{9,10},{10,1... | collective-permute-start | bytes 786440 | tf_op jit(solution)/shard_map/ppermute | solution.py:65
  145.5 21.3 %collective-permute-start.25 = (bf16[128,1024]{1,0:T(8,128)(2,1)S(1)}, bf16[128,1024]{1,0:T(8,128)(2,1)S(1)}, u32[]{:S(2)}, u32[]{:S(2)}) collective-permute-start(bf16[128,1024]{1,0:T(8,128)(2,1)S(1)} %get-tuple-element.45.refs_4_.refs_0_), channel_id=1, source_target_pairs={{0,2},{1,3},{2,0},{3,1},{4,6},{5,7},{6,4},{7,5},{8,10},{9,11},{10,... | collective-permute-start | bytes 786440 | tf_op jit(solution)/shard_map/ppermute | solution.py:65
  146.0 20.8 %collective-permute-start.26 = (bf16[128,1024]{1,0:T(8,128)(2,1)S(1)}, bf16[128,1024]{1,0:T(8,128)(2,1)S(1)}, u32[]{:S(2)}, u32[]{:S(2)}) collective-permute-start(bf16[128,1024]{1,0:T(8,128)(2,1)S(1)} %get-tuple-element.45.refs_4_.refs_0_), channel_id=1, source_target_pairs={{0,3},{1,0},{2,1},{3,2},{4,7},{5,4},{6,5},{7,6},{8,11},{9,8},{10,9... | collective-permute-start | bytes 786440 | tf_op jit(solution)/shard_map/ppermute | solution.py:65
  150.4 14.8 %collective-permute-start.22 = (bf16[2,64,1024]{2,1,0:T(8,128)(2,1)S(1)}, bf16[2,64,1024]{2,1,0:T(8,128)(2,1)S(1)}, u32[]{:S(2)}, u32[]{:S(2)}) collective-permute-start(bf16[2,64,1024]{2,1,0:T(8,128)(2,1)S(1)} %shard_map.67.refs_8_), channel_id=1, source_target_pairs={{0,8},{4,12},{8,0},{12,4},{1,9},{5,13},{9,1},{13,5},{2,10},{6,14},... | collective-permute-start | bytes 786440 | tf_op jit(solution)/shard_map/ppermute | solution.py:260
  169.4 42.1 %collective-permute-start.30 = (bf16[4,1024,1024]{2,1,0:T(8,128)(2,1)}, bf16[4,1024,1024]{2,1,0:T(8,128)(2,1)}, u32[]{:S(2)}, u32[]{:S(2)}) collective-permute-start(bf16[4,1024,1024]{2,1,0:T(8,128)(2,1)} %shard_map.65.refs_0_.refs_6_), channel_id=1, source_target_pairs={{0,4},{4,0},{8,12},{12,8},{1,5},{5,1},{9,13},{13,9},{2,6},{6,2},{1... | collective-permute-start | bytes 25165832 | tf_op jit(solution)/shard_map/ppermute | solution.py:218
  169.5 27.1 %collective-permute-start.21 = (bf16[4,128,1024]{2,1,0:T(8,128)(2,1)}, bf16[4,128,1024]{2,1,0:T(8,128)(2,1)S(1)}, u32[]{:S(2)}, u32[]{:S(2)}) collective-permute-start(bf16[4,128,1024]{2,1,0:T(8,128)(2,1)} %get-tuple-element.46.refs_0_), channel_id=1, source_target_pairs={{0,8},{4,12},{8,0},{12,4},{1,9},{5,13},{9,1},{13,5},{2,10},{6,14},... | collective-permute-start | bytes 3145736 | tf_op jit(solution)/shard_map/ppermute | solution.py:272
  170.7 28.2 %collective-permute-start.31 = (bf16[128,1024]{1,0:T(8,128)(2,1)}, bf16[128,1024]{1,0:T(8,128)(2,1)S(1)}, u32[]{:S(2)}, u32[]{:S(2)}) collective-permute-start(bf16[128,1024]{1,0:T(8,128)(2,1)} %get-tuple-element.49.refs_4_.refs_0_), channel_id=1, source_target_pairs={{0,1},{1,2},{2,3},{3,0},{4,5},{5,6},{6,7},{7,4},{8,9},{9,10},{10,1... | collective-permute-start | bytes 786440 | tf_op jit(solution)/shard_map/ppermute | solution.py:65
  173.1 25.8 %collective-permute-start.32 = (bf16[128,1024]{1,0:T(8,128)(2,1)}, bf16[128,1024]{1,0:T(8,128)(2,1)S(1)}, u32[]{:S(2)}, u32[]{:S(2)}) collective-permute-start(bf16[128,1024]{1,0:T(8,128)(2,1)} %get-tuple-element.49.refs_4_.refs_0_), channel_id=1, source_target_pairs={{0,2},{1,3},{2,0},{3,1},{4,6},{5,7},{6,4},{7,5},{8,10},{9,11},{10,... | collective-permute-start | bytes 786440 | tf_op jit(solution)/shard_map/ppermute | solution.py:65
  175.5 23.4 %collective-permute-start.33 = (bf16[128,1024]{1,0:T(8,128)(2,1)}, bf16[128,1024]{1,0:T(8,128)(2,1)S(1)}, u32[]{:S(2)}, u32[]{:S(2)}) collective-permute-start(bf16[128,1024]{1,0:T(8,128)(2,1)} %get-tuple-element.49.refs_4_.refs_0_), channel_id=1, source_target_pairs={{0,3},{1,0},{2,1},{3,2},{4,7},{5,4},{6,5},{7,6},{8,11},{9,8},{10,9... | collective-permute-start | bytes 786440 | tf_op jit(solution)/shard_map/ppermute | solution.py:65
  196.6 10.6 %collective-permute-start.29 = (bf16[2,64,1024]{2,1,0:T(8,128)(2,1)}, bf16[2,64,1024]{2,1,0:T(8,128)(2,1)}, u32[]{:S(2)}, u32[]{:S(2)}) collective-permute-start(bf16[2,64,1024]{2,1,0:T(8,128)(2,1)} %collective-permute-done.28.refs_4_), channel_id=1, source_target_pairs={{0,1},{1,0},{2,3},{3,2},{4,5},{5,4},{6,7},{7,6},{8,9},{9,8},{10,11... | collective-permute-start | bytes 786440 | tf_op jit(solution)/shard_map/ppermute | solution.py:264
  201.3 8.3 %collective-permute-start.35 = (bf16[2,64,1024]{2,1,0:T(8,128)(2,1)}, bf16[2,64,1024]{2,1,0:T(8,128)(2,1)}, u32[]{:S(2)}, u32[]{:S(2)}) collective-permute-start(bf16[2,64,1024]{2,1,0:T(8,128)(2,1)} %shard_map.73.refs_8_), channel_id=1, source_target_pairs={{0,8},{4,12},{8,0},{12,4},{1,9},{5,13},{9,1},{13,5},{2,10},{6,14},... | collective-permute-start | bytes 786440 | tf_op jit(solution)/shard_map/ppermute | solution.py:260
  204.9 25.6 %collective-permute-start.27 = (bf16[4,128,1024]{2,1,0:T(8,128)(2,1)S(1)}, bf16[4,128,1024]{2,1,0:T(8,128)(2,1)S(1)}, u32[]{:S(2)}, u32[]{:S(2)}) collective-permute-start(bf16[4,128,1024]{2,1,0:T(8,128)(2,1)S(1)} %get-tuple-element.50.refs_0_), channel_id=1, source_target_pairs={{0,8},{4,12},{8,0},{12,4},{1,9},{5,13},{9,1},{13,5},{2,10},{6,14},... | collective-permute-start | bytes 3145736 | tf_op jit(solution)/shard_map/ppermute | solution.py:272
  206.2 26.6 %collective-permute-start.37 = (bf16[128,1024]{1,0:T(8,128)(2,1)}, bf16[128,1024]{1,0:T(8,128)(2,1)S(1)}, u32[]{:S(2)}, u32[]{:S(2)}) collective-permute-start(bf16[128,1024]{1,0:T(8,128)(2,1)} %copy-done.8), channel_id=1, source_target_pairs={{0,1},{1,2},{2,3},{3,0},{4,5},{5,6},{6,7},{7,4},{8,9},{9,10},{10,1... | collective-permute-start | bytes 786440 | tf_op jit(solution)/shard_map/ppermute | solution.py:65
  207.2 26.2 %collective-permute-start.38 = (bf16[128,1024]{1,0:T(8,128)(2,1)}, bf16[128,1024]{1,0:T(8,128)(2,1)S(1)}, u32[]{:S(2)}, u32[]{:S(2)}) collective-permute-start(bf16[128,1024]{1,0:T(8,128)(2,1)} %copy-done.8), channel_id=1, source_target_pairs={{0,2},{1,3},{2,0},{3,1},{4,6},{5,7},{6,4},{7,5},{8,10},{9,11},{10,... | collective-permute-start | bytes 786440 | tf_op jit(solution)/shard_map/ppermute | solution.py:65
  209.5 25.6 %collective-permute-start.39 = (bf16[128,1024]{1,0:T(8,128)(2,1)}, bf16[128,1024]{1,0:T(8,128)(2,1)S(1)}, u32[]{:S(2)}, u32[]{:S(2)}) collective-permute-start(bf16[128,1024]{1,0:T(8,128)(2,1)} %copy-done.8), channel_id=1, source_target_pairs={{0,3},{1,0},{2,1},{3,2},{4,7},{5,4},{6,5},{7,6},{8,11},{9,8},{10,9... | collective-permute-start | bytes 786440 | tf_op jit(solution)/shard_map/ppermute | solution.py:65
  211.4 26.6 %collective-permute-start.36 = (bf16[2,64,1024]{2,1,0:T(8,128)(2,1)}, bf16[2,64,1024]{2,1,0:T(8,128)(2,1)S(1)}, u32[]{:S(2)}, u32[]{:S(2)}) collective-permute-start(bf16[2,64,1024]{2,1,0:T(8,128)(2,1)} %collective-permute-done.35.refs_4_), channel_id=1, source_target_pairs={{0,1},{1,0},{2,3},{3,2},{4,5},{5,4},{6,7},{7,6},{8,9},{9,8},{10,11... | collective-permute-start | bytes 786440 | tf_op jit(solution)/shard_map/ppermute | solution.py:264
  230.5 26.1 %collective-permute-start.34 = (bf16[4,128,1024]{2,1,0:T(8,128)(2,1)S(1)}, bf16[4,128,1024]{2,1,0:T(8,128)(2,1)S(1)}, u32[]{:S(2)}, u32[]{:S(2)}) collective-permute-start(bf16[4,128,1024]{2,1,0:T(8,128)(2,1)S(1)} %get-tuple-element.54.refs_0_), channel_id=1, source_target_pairs={{0,8},{4,12},{8,0},{12,4},{1,9},{5,13},{9,1},{13,5},{2,10},{6,14},... | collective-permute-start | bytes 3145736 | tf_op jit(solution)/shard_map/ppermute | solution.py:272
  232.8 24.3 %collective-permute-start.43 = (bf16[128,1024]{1,0:T(8,128)(2,1)S(1)}, bf16[128,1024]{1,0:T(8,128)(2,1)S(1)}, u32[]{:S(2)}, u32[]{:S(2)}) collective-permute-start(bf16[128,1024]{1,0:T(8,128)(2,1)S(1)} %get-tuple-element.57.refs_4_.refs_0_), channel_id=1, source_target_pairs={{0,1},{1,2},{2,3},{3,0},{4,5},{5,6},{6,7},{7,4},{8,9},{9,10},{10,1... | collective-permute-start | bytes 786440 | tf_op jit(solution)/shard_map/ppermute | solution.py:65
  233.4 23.7 %collective-permute-start.44 = (bf16[128,1024]{1,0:T(8,128)(2,1)S(1)}, bf16[128,1024]{1,0:T(8,128)(2,1)S(1)}, u32[]{:S(2)}, u32[]{:S(2)}) collective-permute-start(bf16[128,1024]{1,0:T(8,128)(2,1)S(1)} %get-tuple-element.57.refs_4_.refs_0_), channel_id=1, source_target_pairs={{0,2},{1,3},{2,0},{3,1},{4,6},{5,7},{6,4},{7,5},{8,10},{9,11},{10,... | collective-permute-start | bytes 786440 | tf_op jit(solution)/shard_map/ppermute | solution.py:65
  235.2 22.0 %collective-permute-start.45 = (bf16[128,1024]{1,0:T(8,128)(2,1)S(1)}, bf16[128,1024]{1,0:T(8,128)(2,1)S(1)}, u32[]{:S(2)}, u32[]{:S(2)}) collective-permute-start(bf16[128,1024]{1,0:T(8,128)(2,1)S(1)} %get-tuple-element.57.refs_4_.refs_0_), channel_id=1, source_target_pairs={{0,3},{1,0},{2,1},{3,2},{4,7},{5,4},{6,5},{7,6},{8,11},{9,8},{10,9... | collective-permute-start | bytes 786440 | tf_op jit(solution)/shard_map/ppermute | solution.py:65
  238.1 23.8 %collective-permute-start.41 = (bf16[2,64,1024]{2,1,0:T(8,128)(2,1)S(1)}, bf16[2,64,1024]{2,1,0:T(8,128)(2,1)}, u32[]{:S(2)}, u32[]{:S(2)}) collective-permute-start(bf16[2,64,1024]{2,1,0:T(8,128)(2,1)S(1)} %shard_map.76.refs_8_), channel_id=1, source_target_pairs={{0,8},{4,12},{8,0},{12,4},{1,9},{5,13},{9,1},{13,5},{2,10},{6,14},... | collective-permute-start | bytes 786440 | tf_op jit(solution)/shard_map/ppermute | solution.py:260
  259.6 9.2 %collective-permute-start.47 = (bf16[2,64,1024]{2,1,0:T(8,128)(2,1)}, bf16[2,64,1024]{2,1,0:T(8,128)(2,1)}, u32[]{:S(2)}, u32[]{:S(2)}) collective-permute-start(bf16[2,64,1024]{2,1,0:T(8,128)(2,1)} %shard_map.79.refs_8_), channel_id=1, source_target_pairs={{0,8},{4,12},{8,0},{12,4},{1,9},{5,13},{9,1},{13,5},{2,10},{6,14},... | collective-permute-start | bytes 786440 | tf_op jit(solution)/shard_map/ppermute | solution.py:260
  261.9 9.2 %collective-permute-start.42 = (bf16[2,64,1024]{2,1,0:T(8,128)(2,1)}, bf16[2,64,1024]{2,1,0:T(8,128)(2,1)}, u32[]{:S(2)}, u32[]{:S(2)}) collective-permute-start(bf16[2,64,1024]{2,1,0:T(8,128)(2,1)} %collective-permute-done.41.refs_4_), channel_id=1, source_target_pairs={{0,1},{1,0},{2,3},{3,2},{4,5},{5,4},{6,7},{7,6},{8,9},{9,8},{10,11... | collective-permute-start | bytes 786440 | tf_op jit(solution)/shard_map/ppermute | solution.py:264
  262.1 29.1 %collective-permute-start.40 = (bf16[4,128,1024]{2,1,0:T(8,128)(2,1)S(1)}, bf16[4,128,1024]{2,1,0:T(8,128)(2,1)S(1)}, u32[]{:S(2)}, u32[]{:S(2)}) collective-permute-start(bf16[4,128,1024]{2,1,0:T(8,128)(2,1)S(1)} %get-tuple-element.58.refs_0_), channel_id=1, source_target_pairs={{0,8},{4,12},{8,0},{12,4},{1,9},{5,13},{9,1},{13,5},{2,10},{6,14},... | collective-permute-start | bytes 3145736 | tf_op jit(solution)/shard_map/ppermute | solution.py:272
  268.8 22.9 %collective-permute-start.48 = (bf16[2,64,1024]{2,1,0:T(8,128)(2,1)}, bf16[2,64,1024]{2,1,0:T(8,128)(2,1)S(1)}, u32[]{:S(2)}, u32[]{:S(2)}) collective-permute-start(bf16[2,64,1024]{2,1,0:T(8,128)(2,1)} %collective-permute-done.47.refs_4_), channel_id=1, source_target_pairs={{0,1},{1,0},{2,3},{3,2},{4,5},{5,4},{6,7},{7,6},{8,9},{9,8},{10,11... | collective-permute-start | bytes 786440 | tf_op jit(solution)/shard_map/ppermute | solution.py:264
  286.6 27.1 %collective-permute-start.46 = (bf16[4,128,1024]{2,1,0:T(8,128)(2,1)}, bf16[4,128,1024]{2,1,0:T(8,128)(2,1)}, u32[]{:S(2)}, u32[]{:S(2)}) collective-permute-start(bf16[4,128,1024]{2,1,0:T(8,128)(2,1)} %get-tuple-element.62.refs_0_), channel_id=1, source_target_pairs={{0,8},{4,12},{8,0},{12,4},{1,9},{5,13},{9,1},{13,5},{2,10},{6,14},... | collective-permute-start | bytes 3145736 | tf_op jit(solution)/shard_map/ppermute | solution.py:272
  303.6 30.0 %collective-permute-start.49 = (bf16[4,128,1024]{2,1,0:T(8,128)(2,1)}, bf16[4,128,1024]{2,1,0:T(8,128)(2,1)S(1)}, u32[]{:S(2)}, u32[]{:S(2)}) collective-permute-start(bf16[4,128,1024]{2,1,0:T(8,128)(2,1)} %get-tuple-element.66.refs_0_), channel_id=1, source_target_pairs={{0,8},{4,12},{8,0},{12,4},{1,9},{5,13},{9,1},{13,5},{2,10},{6,14},... | collective-permute-start | bytes 3145736 | tf_op jit(solution)/shard_map/ppermute | solution.py:272
  (95 other events, 746.9 us)

commit v3 on v2

--- a/solution.py
+++ b/solution.py
@@ -304,7 +304,8 @@
             start_gather(tick + 2)
             start_cross(tick + 1)
         multiply(tick)
-        relay(tick)
+        if tick > 1:
+            relay(tick - 1)
         start_swap(tick + 1)
     finish(count - 1)
 

time: 345 us -> 343 us (level)
  local copies, waits for them, and re-layouts: 36.3 us -> 31.1 us
    unnamed x188 -> x186, local copies, waits for them, and re-layouts: 34.1 us -> 28.9 us
  transfers between devices with their start and end apart: 53 -> 53, of which waited for: 20 -> 19; matrix products, arithmetic and copies ran while one was open for 3% -> 3% of each run, Pallas kernels for 31% -> 31%
where the time goes in v3:
time: 343 us; the launch traced here: 342 us
  Pallas kernels  119 us (35%)
  waiting for transfers between devices  104 us (30%)
  starting transfers between devices  78 us (23%)
  local copies, waits for them, and re-layouts  31.1 us (9%)
  other arithmetic  7.97 us (2%)
    pallas_call x8, Pallas kernels, partials(): pl.pallas_call(kernel, grid_spec=pltpu.PrefetchScalarGridSpec(num_scalar_...  82.8 us
    ppermute x8, waiting for transfers between devices, multiply(): received[j] = lax.ppermute(sent, 'samp', across)  44 us
    ppermute x24, starting transfers between devices, gather(): lax.ppermute(block, 'bond', [(i, (i + d) % bond) for i in range(bond)])  37.5 us
    unnamed x186, local copies, waits for them, and re-layouts  28.9 us
    ppermute x24, waiting for transfers between devices, gather(): lax.ppermute(block, 'bond', [(i, (i + d) % bond) for i in range(bond)])  25 us
    pallas_call x2, Pallas kernels, outcome_major(): pl.pallas_call(kernel, grid=(rows // tile,), in_specs=[pl.BlockSpec((1, 1...  20.2 us
    ppermute x8, waiting for transfers between devices, start_swap(): halves[j].append(lax.ppermute(halves[j][0], 'bond', beside))  17.1 us
    ppermute x8, starting transfers between devices, start_swap(): halves[j].append(lax.ppermute(halves[j][0], 'bond', beside))  16.3 us
  transfers between devices with their start and end apart: 53, of which 19 were waited for; matrix products, arithmetic and copies ran while one was open for 3% of the time, Pallas kernels for 31%

profile of v3, /device:TPU:0, one launch (start us, length us, event | category | flops | bytes accessed | tf_op | source)
XLA Modules:
  0.0 341.8 jit_solution(12738165919707431360)
XLA Ops:
  0.6 9.8 %shard_map.60.refs_6_ = bf16[4,1024,1024]{2,1,0:T(8,128)(2,1)} custom-call(bf16[2,1,1024,4,1024]{4,3,2,1,0:T(4,128)(2,1)} %source.3), custom_call_target="tpu_custom_call" | custom-call | bytes 335544320 | tf_op jit(solution)/shard_map/pallas_call | solution.py:43
  11.8 2.6 collective-permute-start
  14.3 2.6 collective-permute-start.1
  20.4 3.3 collective-permute-done.refs_1_
  23.7 11.0 %collective-permute-done.1.refs_2_ = bf16[128,1024]{1,0:T(8,128)(2,1)S(1)} collective-permute-done((bf16[128,1024]{1,0:T(8,128)(2,1)S(1)}, bf16[128,1024]{1,0:T(8,128)(2,1)S(1)}, u32[]{:S(2)}, u32[]{:S(2)}) %collective-permute-start.1) | collective-permute-done | bytes 262176 | tf_op jit(solution)/shard_map/ppermute | solution.py:65
  37.9 6.0 %collective-permute-done.3.refs_4_ = bf16[2,64,1024]{2,1,0:T(8,128)(2,1)S(1)} collective-permute-done((bf16[2,64,1024]{2,1,0:T(8,128)(2,1)S(1)}, bf16[2,64,1024]{2,1,0:T(8,128)(2,1)S(1)}, u32[]{:S(2)}, u32[]{:S(2)}) %collective-permute-start.3) | collective-permute-done | bytes 262176 | tf_op jit(solution)/shard_map/ppermute | solution.py:260
  43.9 6.2 %collective-permute-start.4 = (bf16[2,64,1024]{2,1,0:T(8,128)(2,1)S(1)}, bf16[2,64,1024]{2,1,0:T(8,128)(2,1)S(1)}, u32[]{:S(2)}, u32[]{:S(2)}) collective-permute-start(bf16[2,64,1024]{2,1,0:T(8,128)(2,1)S(1)} %collective-permute-done.3.refs_4_), channel_id=1, source_target_pairs={{0,1},{1,0},{2,3},{3,2},{4,5},{5,4},{6,7},{7,6},{8,9},{9,8},{10,11... | collective-permute-start | bytes 786440 | tf_op jit(solution)/shard_map/ppermute | solution.py:264
  53.5 2.9 collective-permute-start.9
  56.4 7.3 %collective-permute-done.4.refs_5_ = bf16[2,64,1024]{2,1,0:T(8,128)(2,1)S(1)} collective-permute-done((bf16[2,64,1024]{2,1,0:T(8,128)(2,1)S(1)}, bf16[2,64,1024]{2,1,0:T(8,128)(2,1)S(1)}, u32[]{:S(2)}, u32[]{:S(2)}) %collective-permute-start.4) | collective-permute-done | bytes 262176 | tf_op jit(solution)/shard_map/ppermute | solution.py:264
  71.1 9.2 %shard_map.61 = (f32[4,128,1024]{2,1,0:T(8,128)S(1)}, bf16[4,128,1024]{2,1,0:T(8,128)(2,1)S(1)}) custom-call(s32[4]{0:T(128)S(1)} %add_add_fusion.1.places_ref, bf16[128,1024]{1,0:T(8,128)(2,1)S(1)} %copy-done.8, bf16[128,1024]{1,0:T(8,128)(2,1)S(1)} %copy-done.20, bf16[128,1024]{1,0:T(8,128)(2,1)S(1)} %copy-done.22, bf16[128,1024]{1,0:T(8,128)(2,1)S(1)} %copy-done.24, ...), custom_call_target="tpu_custom_call" | custom-call | flops 85899345920 | bytes 199229440 | tf_op jit(solution)/shard_map/pallas_call | solution.py:144
  81.6 3.6 %collective-permute-start.14 = (bf16[128,1024]{1,0:T(8,128)(2,1)S(1)}, bf16[128,1024]{1,0:T(8,128)(2,1)S(1)}, u32[]{:S(2)}, u32[]{:S(2)}) collective-permute-start(bf16[128,1024]{1,0:T(8,128)(2,1)S(1)} %copy-done.15), channel_id=1, source_target_pairs={{0,3},{1,0},{2,1},{3,2},{4,7},{5,4},{6,5},{7,6},{8,11},{9,8},{10,9... | collective-permute-start | bytes 786440 | tf_op jit(solution)/shard_map/ppermute | solution.py:65
  86.6 3.0 collective-permute-done.12.refs_1_
  89.7 7.6 %collective-permute-done.13.refs_2_ = bf16[128,1024]{1,0:T(8,128)(2,1)S(1)} collective-permute-done((bf16[128,1024]{1,0:T(8,128)(2,1)S(1)}, bf16[128,1024]{1,0:T(8,128)(2,1)S(1)}, u32[]{:S(2)}, u32[]{:S(2)}) %collective-permute-start.13) | collective-permute-done | bytes 262176 | tf_op jit(solution)/shard_map/ppermute | solution.py:65
  97.3 1.7 shard_map.63.refs_8_
  100.6 3.4 collective-permute-start.11
  106.8 3.0 collective-permute-start.19
  109.8 9.8 %collective-permute-done.11.refs_5_ = bf16[2,64,1024]{2,1,0:T(8,128)(2,1)} collective-permute-done((bf16[2,64,1024]{2,1,0:T(8,128)(2,1)}, bf16[2,64,1024]{2,1,0:T(8,128)(2,1)}, u32[]{:S(2)}, u32[]{:S(2)}) %collective-permute-start.11) | collective-permute-done | bytes 262176 | tf_op jit(solution)/shard_map/ppermute | solution.py:264
  119.6 2.0 collective-permute-start.17
  124.5 10.5 %shard_map.64 = (f32[4,128,1024]{2,1,0:T(8,128)S(1)}, bf16[4,128,1024]{2,1,0:T(8,128)(2,1)S(1)}) custom-call(s32[4]{0:T(128)S(1)} %add_add_fusion.1.places_ref, bf16[128,1024]{1,0:T(8,128)(2,1)S(1)} %get-tuple-element.39.refs_0_, bf16[128,1024]{1,0:T(8,128)(2,1)S(1)} %copy-done.26, bf16[128,1024]{1,0:T(8,128)(2,1)S(1)} %copy-done.28, ...), custom_call_target="tpu_custom_call" | custom-call | flops 85899345920 | bytes 199229440 | tf_op jit(solution)/shard_map/pallas_call | solution.py:144
  136.7 2.9 collective-permute-start.26
  140.6 2.0 collective-permute-start.22
  142.7 10.4 %shard_map.67 = (f32[4,128,1024]{2,1,0:T(8,128)S(1)}, bf16[4,128,1024]{2,1,0:T(8,128)(2,1)S(1)}) custom-call(s32[4]{0:T(128)S(1)} %add_add_fusion.1.places_ref, bf16[128,1024]{1,0:T(8,128)(2,1)S(1)} %copy-done.16, bf16[128,1024]{1,0:T(8,128)(2,1)S(1)} %copy-done.52, bf16[128,1024]{1,0:T(8,128)(2,1)S(1)} %copy-done.56, bf16[128,1024]{1,0:T(8,128)(2,1)S(1)} %copy-done.58, ...), custom_call_target="tpu_custom_call" | custom-call | flops 85899345920 | bytes 199229440 | tf_op jit(solution)/shard_map/pallas_call | solution.py:144
  153.1 10.4 %shard_map.68.refs_0_.refs_6_ = bf16[4,1024,1024]{2,1,0:T(8,128)(2,1)} custom-call(bf16[2,1,1024,4,1024]{4,3,2,1,0:T(4,128)(2,1)} %source.3, bf16[4,128,1024]{2,1,0:T(8,128)(2,1)S(1)} %get-tuple-element.46.refs_0_), custom_call_target="tpu_custom_call" | custom-call | bytes 335544320 | tf_op jit(solution)/shard_map/pallas_call | solution.py:43
  167.4 2.0 collective-permute-start.21
  171.6 2.0 collective-permute-start.32
  175.0 2.9 collective-permute-start.33
  184.6 9.1 %shard_map.71 = (f32[4,128,1024]{2,1,0:T(8,128)S(1)}, bf16[4,128,1024]{2,1,0:T(8,128)(2,1)S(1)}) custom-call(s32[4]{0:T(128)S(1)} %add_add_fusion.1.places_ref, bf16[128,1024]{1,0:T(8,128)(2,1)S(1)} %copy-done.14, bf16[128,1024]{1,0:T(8,128)(2,1)S(1)} %copy-done.42, bf16[128,1024]{1,0:T(8,128)(2,1)S(1)} %copy-done.46, bf16[128,1024]{1,0:T(8,128)(2,1)S(1)} %copy-done.50, ...), custom_call_target="tpu_custom_call" | custom-call | flops 85899345920 | bytes 199229440 | tf_op jit(solution)/shard_map/pallas_call | solution.py:144
  204.0 1.7 collective-permute-start.38
  205.6 3.1 collective-permute-done.35.refs_4_
  208.7 2.2 collective-permute-start.39
  211.8 10.5 %shard_map.74 = (f32[4,128,1024]{2,1,0:T(8,128)S(1)}, bf16[4,128,1024]{2,1,0:T(8,128)(2,1)S(1)}) custom-call(s32[4]{0:T(128)S(1)} %add_add_fusion.2.places_ref, bf16[128,1024]{1,0:T(8,128)(2,1)S(1)} %get-tuple-element.45.refs_4_.refs_0_, bf16[128,1024]{1,0:T(8,128)(2,1)S(1)} %copy-done.34, bf16[128,1024]{1,0:T(8,128)(2,1)S(1)} %copy-done.36, ...), custom_call_target="tpu_custom_call" | custom-call | flops 85899345920 | bytes 199229440 | tf_op jit(solution)/shard_map/pallas_call | solution.py:144
  222.4 6.2 %collective-permute-done.27.received_ref = bf16[4,128,1024]{2,1,0:T(8,128)(2,1)S(1)} collective-permute-done((bf16[4,128,1024]{2,1,0:T(8,128)(2,1)}, bf16[4,128,1024]{2,1,0:T(8,128)(2,1)S(1)}, u32[]{:S(2)}, u32[]{:S(2)}) %collective-permute-start.27) | collective-permute-done | bytes 1048608 | tf_op jit(solution)/shard_map/ppermute | solution.py:272
  228.6 1.7 collective-permute-start.34
  232.8 2.8 collective-permute-start.45
  237.0 10.5 %shard_map.77 = (f32[4,128,1024]{2,1,0:T(8,128)S(1)}, bf16[4,128,1024]{2,1,0:T(8,128)(2,1)S(1)}) custom-call(s32[4]{0:T(128)S(1)} %add_add_fusion.2.places_ref, bf16[128,1024]{1,0:T(8,128)(2,1)} %get-tuple-element.49.refs_4_.refs_0_, bf16[128,1024]{1,0:T(8,128)(2,1)S(1)} %copy-done.40, bf16[128,1024]{1,0:T(8,128)(2,1)S(1)} %copy-done.44, ...), custom_call_target="tpu_custom_call" | custom-call | flops 85899345920 | bytes 199229440 | tf_op jit(solution)/shard_map/pallas_call | solution.py:144
  247.5 7.2 %collective-permute-done.34.received_ref = bf16[4,128,1024]{2,1,0:T(8,128)(2,1)S(1)} collective-permute-done((bf16[4,128,1024]{2,1,0:T(8,128)(2,1)S(1)}, bf16[4,128,1024]{2,1,0:T(8,128)(2,1)S(1)}, u32[]{:S(2)}, u32[]{:S(2)}) %collective-permute-start.34) | collective-permute-done | bytes 1048608 | tf_op jit(solution)/shard_map/ppermute | solution.py:272
  257.8 1.7 collective-permute-start.47
  260.2 1.8 collective-permute-start.40
  262.0 4.9 %collective-permute-done.47.refs_4_ = bf16[2,64,1024]{2,1,0:T(8,128)(2,1)} collective-permute-done((bf16[2,64,1024]{2,1,0:T(8,128)(2,1)}, bf16[2,64,1024]{2,1,0:T(8,128)(2,1)}, u32[]{:S(2)}, u32[]{:S(2)}) %collective-permute-start.47) | collective-permute-done | bytes 262176 | tf_op jit(solution)/shard_map/ppermute | solution.py:260
  266.9 2.5 collective-permute-start.48
  272.2 11.3 %shard_map.80 = (f32[4,128,1024]{2,1,0:T(8,128)S(1)}, bf16[4,128,1024]{2,1,0:T(8,128)(2,1)}) custom-call(s32[4]{0:T(128)S(1)} %add_add_fusion.2.places_ref, bf16[128,1024]{1,0:T(8,128)(2,1)S(1)} %copy-done.10, bf16[128,1024]{1,0:T(8,128)(2,1)S(1)} %copy-done.54, bf16[128,1024]{1,0:T(8,128)(2,1)S(1)} %copy-done.60, bf16[128,1024]{1,0:T(8,128)(2,1)S(1)} %copy-done.62, ...), custom_call_target="tpu_custom_call" | custom-call | flops 85899345920 | bytes 199229440 | tf_op jit(solution)/shard_map/pallas_call | solution.py:144
  285.1 4.1 %collective-permute-done.40.received_ref = bf16[4,128,1024]{2,1,0:T(8,128)(2,1)S(1)} collective-permute-done((bf16[4,128,1024]{2,1,0:T(8,128)(2,1)S(1)}, bf16[4,128,1024]{2,1,0:T(8,128)(2,1)S(1)}, u32[]{:S(2)}, u32[]{:S(2)}) %collective-permute-start.40) | collective-permute-done | bytes 1048608 | tf_op jit(solution)/shard_map/ppermute | solution.py:272
  290.4 11.3 %shard_map.82 = (f32[4,128,1024]{2,1,0:T(8,128)S(1)}, bf16[4,128,1024]{2,1,0:T(8,128)(2,1)}) custom-call(s32[4]{0:T(128)S(1)} %add_add_fusion.2.places_ref, bf16[128,1024]{1,0:T(8,128)(2,1)S(1)} %copy-done.12, bf16[128,1024]{1,0:T(8,128)(2,1)S(1)} %copy-done.64, bf16[128,1024]{1,0:T(8,128)(2,1)S(1)} %copy-done.66, bf16[128,1024]{1,0:T(8,128)(2,1)S(1)} %copy-done.68, ...), custom_call_target="tpu_custom_call" | custom-call | flops 85899345920 | bytes 199229440 | tf_op jit(solution)/shard_map/pallas_call | solution.py:144
  303.4 8.4 %collective-permute-done.46.received_ref = bf16[4,128,1024]{2,1,0:T(8,128)(2,1)} collective-permute-done((bf16[4,128,1024]{2,1,0:T(8,128)(2,1)}, bf16[4,128,1024]{2,1,0:T(8,128)(2,1)}, u32[]{:S(2)}, u32[]{:S(2)}) %collective-permute-start.46) | collective-permute-done | bytes 1048608 | tf_op jit(solution)/shard_map/ppermute | solution.py:272
  313.4 1.7 shard_map.83
  315.2 16.6 %collective-permute-done.49.received_ref = bf16[4,128,1024]{2,1,0:T(8,128)(2,1)S(1)} collective-permute-done((bf16[4,128,1024]{2,1,0:T(8,128)(2,1)}, bf16[4,128,1024]{2,1,0:T(8,128)(2,1)S(1)}, u32[]{:S(2)}, u32[]{:S(2)}) %collective-permute-start.49) | collective-permute-done | bytes 1048608 | tf_op jit(solution)/shard_map/ppermute | solution.py:272
  332.3 2.5 collective-permute-start.50
  334.8 2.4 collective-permute-start.52
  (301 shorter events, 77.8 us)
Async XLA Ops:
  10.4 54.0 %collective-permute-start.5 = (bf16[4,1024,1024]{2,1,0:T(8,128)(2,1)}, bf16[4,1024,1024]{2,1,0:T(8,128)(2,1)}, u32[]{:S(2)}, u32[]{:S(2)}) collective-permute-start(bf16[4,1024,1024]{2,1,0:T(8,128)(2,1)} %shard_map.60.refs_6_), channel_id=1, source_target_pairs={{0,4},{4,0},{8,12},{12,8},{1,5},{5,1},{9,13},{13,9},{2,6},{6,2},{1... | collective-permute-start | bytes 25165832 | tf_op jit(solution)/shard_map/ppermute | solution.py:218
  11.8 11.9 %collective-permute-start = (bf16[128,1024]{1,0:T(8,128)(2,1)S(1)}, bf16[128,1024]{1,0:T(8,128)(2,1)S(1)}, u32[]{:S(2)}, u32[]{:S(2)}) collective-permute-start(bf16[128,1024]{1,0:T(8,128)(2,1)S(1)} %get-tuple-element.74.refs_0_), channel_id=1, source_target_pairs={{0,1},{1,2},{2,3},{3,0},{4,5},{5,6},{6,7},{7,4},{8,9},{9,10},{10,1... | collective-permute-start | bytes 786440 | tf_op jit(solution)/shard_map/ppermute | solution.py:65
  14.3 20.3 %collective-permute-start.1 = (bf16[128,1024]{1,0:T(8,128)(2,1)S(1)}, bf16[128,1024]{1,0:T(8,128)(2,1)S(1)}, u32[]{:S(2)}, u32[]{:S(2)}) collective-permute-start(bf16[128,1024]{1,0:T(8,128)(2,1)S(1)} %get-tuple-element.74.refs_0_), channel_id=1, source_target_pairs={{0,2},{1,3},{2,0},{3,1},{4,6},{5,7},{6,4},{7,5},{8,10},{9,11},{10,... | collective-permute-start | bytes 786440 | tf_op jit(solution)/shard_map/ppermute | solution.py:65
  16.9 17.8 %collective-permute-start.2 = (bf16[128,1024]{1,0:T(8,128)(2,1)S(1)}, bf16[128,1024]{1,0:T(8,128)(2,1)S(1)}, u32[]{:S(2)}, u32[]{:S(2)}) collective-permute-start(bf16[128,1024]{1,0:T(8,128)(2,1)S(1)} %get-tuple-element.74.refs_0_), channel_id=1, source_target_pairs={{0,3},{1,0},{2,1},{3,2},{4,7},{5,4},{6,5},{7,6},{8,11},{9,8},{10,9... | collective-permute-start | bytes 786440 | tf_op jit(solution)/shard_map/ppermute | solution.py:65
  43.9 19.8 %collective-permute-start.4 = (bf16[2,64,1024]{2,1,0:T(8,128)(2,1)S(1)}, bf16[2,64,1024]{2,1,0:T(8,128)(2,1)S(1)}, u32[]{:S(2)}, u32[]{:S(2)}) collective-permute-start(bf16[2,64,1024]{2,1,0:T(8,128)(2,1)S(1)} %collective-permute-done.3.refs_4_), channel_id=1, source_target_pairs={{0,1},{1,0},{2,3},{3,2},{4,5},{5,4},{6,7},{7,6},{8,9},{9,8},{10,11... | collective-permute-start | bytes 786440 | tf_op jit(solution)/shard_map/ppermute | solution.py:264
  52.2 28.1 %collective-permute-start.7 = (bf16[128,1024]{1,0:T(8,128)(2,1)S(1)}, bf16[128,1024]{1,0:T(8,128)(2,1)S(1)}, u32[]{:S(2)}, u32[]{:S(2)}) collective-permute-start(bf16[128,1024]{1,0:T(8,128)(2,1)S(1)} %get-tuple-element.39.refs_0_), channel_id=1, source_target_pairs={{0,1},{1,2},{2,3},{3,0},{4,5},{5,6},{6,7},{7,4},{8,9},{9,10},{10,1... | collective-permute-start | bytes 786440 | tf_op jit(solution)/shard_map/ppermute | solution.py:65
  52.2 28.1 %collective-permute-start.8 = (bf16[128,1024]{1,0:T(8,128)(2,1)S(1)}, bf16[128,1024]{1,0:T(8,128)(2,1)S(1)}, u32[]{:S(2)}, u32[]{:S(2)}) collective-permute-start(bf16[128,1024]{1,0:T(8,128)(2,1)S(1)} %get-tuple-element.39.refs_0_), channel_id=1, source_target_pairs={{0,2},{1,3},{2,0},{3,1},{4,6},{5,7},{6,4},{7,5},{8,10},{9,11},{10,... | collective-permute-start | bytes 786440 | tf_op jit(solution)/shard_map/ppermute | solution.py:65
  53.5 26.8 %collective-permute-start.9 = (bf16[128,1024]{1,0:T(8,128)(2,1)S(1)}, bf16[128,1024]{1,0:T(8,128)(2,1)S(1)}, u32[]{:S(2)}, u32[]{:S(2)}) collective-permute-start(bf16[128,1024]{1,0:T(8,128)(2,1)S(1)} %get-tuple-element.39.refs_0_), channel_id=1, source_target_pairs={{0,3},{1,0},{2,1},{3,2},{4,7},{5,4},{6,5},{7,6},{8,11},{9,8},{10,9... | collective-permute-start | bytes 786440 | tf_op jit(solution)/shard_map/ppermute | solution.py:65
  81.3 8.4 %collective-permute-start.12 = (bf16[128,1024]{1,0:T(8,128)(2,1)S(1)}, bf16[128,1024]{1,0:T(8,128)(2,1)S(1)}, u32[]{:S(2)}, u32[]{:S(2)}) collective-permute-start(bf16[128,1024]{1,0:T(8,128)(2,1)S(1)} %copy-done.15), channel_id=1, source_target_pairs={{0,1},{1,2},{2,3},{3,0},{4,5},{5,6},{6,7},{7,4},{8,9},{9,10},{10,1... | collective-permute-start | bytes 786440 | tf_op jit(solution)/shard_map/ppermute | solution.py:65
  81.6 15.7 %collective-permute-start.13 = (bf16[128,1024]{1,0:T(8,128)(2,1)S(1)}, bf16[128,1024]{1,0:T(8,128)(2,1)S(1)}, u32[]{:S(2)}, u32[]{:S(2)}) collective-permute-start(bf16[128,1024]{1,0:T(8,128)(2,1)S(1)} %copy-done.15), channel_id=1, source_target_pairs={{0,2},{1,3},{2,0},{3,1},{4,6},{5,7},{6,4},{7,5},{8,10},{9,11},{10,... | collective-permute-start | bytes 786440 | tf_op jit(solution)/shard_map/ppermute | solution.py:65
  81.6 15.7 %collective-permute-start.14 = (bf16[128,1024]{1,0:T(8,128)(2,1)S(1)}, bf16[128,1024]{1,0:T(8,128)(2,1)S(1)}, u32[]{:S(2)}, u32[]{:S(2)}) collective-permute-start(bf16[128,1024]{1,0:T(8,128)(2,1)S(1)} %copy-done.15), channel_id=1, source_target_pairs={{0,3},{1,0},{2,1},{3,2},{4,7},{5,4},{6,5},{7,6},{8,11},{9,8},{10,9... | collective-permute-start | bytes 786440 | tf_op jit(solution)/shard_map/ppermute | solution.py:65
  85.1 15.4 %collective-permute-start.10 = (bf16[2,64,1024]{2,1,0:T(8,128)(2,1)S(1)}, bf16[2,64,1024]{2,1,0:T(8,128)(2,1)}, u32[]{:S(2)}, u32[]{:S(2)}) collective-permute-start(bf16[2,64,1024]{2,1,0:T(8,128)(2,1)S(1)} %shard_map.62.refs_4_), channel_id=1, source_target_pairs={{0,8},{4,12},{8,0},{12,4},{1,9},{5,13},{9,1},{13,5},{2,10},{6,14},... | collective-permute-start | bytes 786440 | tf_op jit(solution)/shard_map/ppermute | solution.py:260
  99.0 20.6 %collective-permute-start.16 = (bf16[2,64,1024]{2,1,0:T(8,128)(2,1)}, bf16[2,64,1024]{2,1,0:T(8,128)(2,1)}, u32[]{:S(2)}, u32[]{:S(2)}) collective-permute-start(bf16[2,64,1024]{2,1,0:T(8,128)(2,1)} %shard_map.63.refs_8_), channel_id=1, source_target_pairs={{0,8},{4,12},{8,0},{12,4},{1,9},{5,13},{9,1},{13,5},{2,10},{6,14},... | collective-permute-start | bytes 786440 | tf_op jit(solution)/shard_map/ppermute | solution.py:260
  100.6 19.0 %collective-permute-start.11 = (bf16[2,64,1024]{2,1,0:T(8,128)(2,1)}, bf16[2,64,1024]{2,1,0:T(8,128)(2,1)}, u32[]{:S(2)}, u32[]{:S(2)}) collective-permute-start(bf16[2,64,1024]{2,1,0:T(8,128)(2,1)} %collective-permute-done.10.refs_4_), channel_id=1, source_target_pairs={{0,1},{1,0},{2,3},{3,2},{4,5},{5,4},{6,7},{7,6},{8,9},{9,8},{10,11... | collective-permute-start | bytes 786440 | tf_op jit(solution)/shard_map/ppermute | solution.py:264
  106.2 28.7 %collective-permute-start.6 = (bf16[4,128,1024]{2,1,0:T(8,128)(2,1)S(1)}, bf16[4,128,1024]{2,1,0:T(8,128)(2,1)S(1)}, u32[]{:S(2)}, u32[]{:S(2)}) collective-permute-start(bf16[4,128,1024]{2,1,0:T(8,128)(2,1)S(1)} %get-tuple-element.38.refs_4_), channel_id=1, source_target_pairs={{0,8},{4,12},{8,0},{12,4},{1,9},{5,13},{9,1},{13,5},{2,10},{6,14},... | collective-permute-start | bytes 3145736 | tf_op jit(solution)/shard_map/ppermute | solution.py:272
  106.8 28.9 %collective-permute-start.18 = (bf16[128,1024]{1,0:T(8,128)(2,1)}, bf16[128,1024]{1,0:T(8,128)(2,1)S(1)}, u32[]{:S(2)}, u32[]{:S(2)}) collective-permute-start(bf16[128,1024]{1,0:T(8,128)(2,1)} %get-tuple-element.44.refs_0_), channel_id=1, source_target_pairs={{0,1},{1,2},{2,3},{3,0},{4,5},{5,6},{6,7},{7,4},{8,9},{9,10},{10,1... | collective-permute-start | bytes 786440 | tf_op jit(solution)/shard_map/ppermute | solution.py:65
  106.8 29.0 %collective-permute-start.19 = (bf16[128,1024]{1,0:T(8,128)(2,1)}, bf16[128,1024]{1,0:T(8,128)(2,1)S(1)}, u32[]{:S(2)}, u32[]{:S(2)}) collective-permute-start(bf16[128,1024]{1,0:T(8,128)(2,1)} %get-tuple-element.44.refs_0_), channel_id=1, source_target_pairs={{0,2},{1,3},{2,0},{3,1},{4,6},{5,7},{6,4},{7,5},{8,10},{9,11},{10,... | collective-permute-start | bytes 786440 | tf_op jit(solution)/shard_map/ppermute | solution.py:65
  119.6 17.1 %collective-permute-start.20 = (bf16[128,1024]{1,0:T(8,128)(2,1)}, bf16[128,1024]{1,0:T(8,128)(2,1)S(1)}, u32[]{:S(2)}, u32[]{:S(2)}) collective-permute-start(bf16[128,1024]{1,0:T(8,128)(2,1)} %get-tuple-element.44.refs_0_), channel_id=1, source_target_pairs={{0,3},{1,0},{2,1},{3,2},{4,7},{5,4},{6,5},{7,6},{8,11},{9,8},{10,9... | collective-permute-start | bytes 786440 | tf_op jit(solution)/shard_map/ppermute | solution.py:65
  119.6 21.0 %collective-permute-start.17 = (bf16[2,64,1024]{2,1,0:T(8,128)(2,1)}, bf16[2,64,1024]{2,1,0:T(8,128)(2,1)S(1)}, u32[]{:S(2)}, u32[]{:S(2)}) collective-permute-start(bf16[2,64,1024]{2,1,0:T(8,128)(2,1)} %collective-permute-done.16.refs_4_), channel_id=1, source_target_pairs={{0,1},{1,0},{2,3},{3,2},{4,5},{5,4},{6,7},{7,6},{8,9},{9,8},{10,11... | collective-permute-start | bytes 786440 | tf_op jit(solution)/shard_map/ppermute | solution.py:264
  135.0 29.2 %collective-permute-start.15 = (bf16[4,128,1024]{2,1,0:T(8,128)(2,1)S(1)}, bf16[4,128,1024]{2,1,0:T(8,128)(2,1)S(1)}, u32[]{:S(2)}, u32[]{:S(2)}) collective-permute-start(bf16[4,128,1024]{2,1,0:T(8,128)(2,1)S(1)} %get-tuple-element.41.refs_0_), channel_id=1, source_target_pairs={{0,8},{4,12},{8,0},{12,4},{1,9},{5,13},{9,1},{13,5},{2,10},{6,14},... | collective-permute-start | bytes 3145736 | tf_op jit(solution)/shard_map/ppermute | solution.py:272
  135.7 29.7 %collective-permute-start.24 = (bf16[128,1024]{1,0:T(8,128)(2,1)S(1)}, bf16[128,1024]{1,0:T(8,128)(2,1)S(1)}, u32[]{:S(2)}, u32[]{:S(2)}) collective-permute-start(bf16[128,1024]{1,0:T(8,128)(2,1)S(1)} %get-tuple-element.45.refs_4_.refs_0_), channel_id=1, source_target_pairs={{0,1},{1,2},{2,3},{3,0},{4,5},{5,6},{6,7},{7,4},{8,9},{9,10},{10,1... | collective-permute-start | bytes 786440 | tf_op jit(solution)/shard_map/ppermute | solution.py:65
  135.7 29.7 %collective-permute-start.25 = (bf16[128,1024]{1,0:T(8,128)(2,1)S(1)}, bf16[128,1024]{1,0:T(8,128)(2,1)S(1)}, u32[]{:S(2)}, u32[]{:S(2)}) collective-permute-start(bf16[128,1024]{1,0:T(8,128)(2,1)S(1)} %get-tuple-element.45.refs_4_.refs_0_), channel_id=1, source_target_pairs={{0,2},{1,3},{2,0},{3,1},{4,6},{5,7},{6,4},{7,5},{8,10},{9,11},{10,... | collective-permute-start | bytes 786440 | tf_op jit(solution)/shard_map/ppermute | solution.py:65
  136.7 28.7 %collective-permute-start.26 = (bf16[128,1024]{1,0:T(8,128)(2,1)S(1)}, bf16[128,1024]{1,0:T(8,128)(2,1)S(1)}, u32[]{:S(2)}, u32[]{:S(2)}) collective-permute-start(bf16[128,1024]{1,0:T(8,128)(2,1)S(1)} %get-tuple-element.45.refs_4_.refs_0_), channel_id=1, source_target_pairs={{0,3},{1,0},{2,1},{3,2},{4,7},{5,4},{6,5},{7,6},{8,11},{9,8},{10,9... | collective-permute-start | bytes 786440 | tf_op jit(solution)/shard_map/ppermute | solution.py:65
  140.6 23.0 %collective-permute-start.22 = (bf16[2,64,1024]{2,1,0:T(8,128)(2,1)S(1)}, bf16[2,64,1024]{2,1,0:T(8,128)(2,1)S(1)}, u32[]{:S(2)}, u32[]{:S(2)}) collective-permute-start(bf16[2,64,1024]{2,1,0:T(8,128)(2,1)S(1)} %shard_map.66.refs_8_), channel_id=1, source_target_pairs={{0,8},{4,12},{8,0},{12,4},{1,9},{5,13},{9,1},{13,5},{2,10},{6,14},... | collective-permute-start | bytes 786440 | tf_op jit(solution)/shard_map/ppermute | solution.py:260
  166.4 8.7 %collective-permute-start.28 = (bf16[2,64,1024]{2,1,0:T(8,128)(2,1)S(1)}, bf16[2,64,1024]{2,1,0:T(8,128)(2,1)}, u32[]{:S(2)}, u32[]{:S(2)}) collective-permute-start(bf16[2,64,1024]{2,1,0:T(8,128)(2,1)S(1)} %shard_map.70.refs_8_), channel_id=1, source_target_pairs={{0,8},{4,12},{8,0},{12,4},{1,9},{5,13},{9,1},{13,5},{2,10},{6,14},... | collective-permute-start | bytes 786440 | tf_op jit(solution)/shard_map/ppermute | solution.py:260
  167.2 43.7 %collective-permute-start.30 = (bf16[4,1024,1024]{2,1,0:T(8,128)(2,1)}, bf16[4,1024,1024]{2,1,0:T(8,128)(2,1)}, u32[]{:S(2)}, u32[]{:S(2)}) collective-permute-start(bf16[4,1024,1024]{2,1,0:T(8,128)(2,1)} %shard_map.68.refs_0_.refs_6_), channel_id=1, source_target_pairs={{0,4},{4,0},{8,12},{12,8},{1,5},{5,1},{9,13},{13,9},{2,6},{6,2},{1... | collective-permute-start | bytes 25165832 | tf_op jit(solution)/shard_map/ppermute | solution.py:218
  167.4 27.9 %collective-permute-start.21 = (bf16[4,128,1024]{2,1,0:T(8,128)(2,1)S(1)}, bf16[4,128,1024]{2,1,0:T(8,128)(2,1)S(1)}, u32[]{:S(2)}, u32[]{:S(2)}) collective-permute-start(bf16[4,128,1024]{2,1,0:T(8,128)(2,1)S(1)} %get-tuple-element.46.refs_0_), channel_id=1, source_target_pairs={{0,8},{4,12},{8,0},{12,4},{1,9},{5,13},{9,1},{13,5},{2,10},{6,14},... | collective-permute-start | bytes 3145736 | tf_op jit(solution)/shard_map/ppermute | solution.py:272
  169.4 28.0 %collective-permute-start.31 = (bf16[128,1024]{1,0:T(8,128)(2,1)}, bf16[128,1024]{1,0:T(8,128)(2,1)S(1)}, u32[]{:S(2)}, u32[]{:S(2)}) collective-permute-start(bf16[128,1024]{1,0:T(8,128)(2,1)} %get-tuple-element.49.refs_4_.refs_0_), channel_id=1, source_target_pairs={{0,1},{1,2},{2,3},{3,0},{4,5},{5,6},{6,7},{7,4},{8,9},{9,10},{10,1... | collective-permute-start | bytes 786440 | tf_op jit(solution)/shard_map/ppermute | solution.py:65
  171.6 25.8 %collective-permute-start.32 = (bf16[128,1024]{1,0:T(8,128)(2,1)}, bf16[128,1024]{1,0:T(8,128)(2,1)S(1)}, u32[]{:S(2)}, u32[]{:S(2)}) collective-permute-start(bf16[128,1024]{1,0:T(8,128)(2,1)} %get-tuple-element.49.refs_4_.refs_0_), channel_id=1, source_target_pairs={{0,2},{1,3},{2,0},{3,1},{4,6},{5,7},{6,4},{7,5},{8,10},{9,11},{10,... | collective-permute-start | bytes 786440 | tf_op jit(solution)/shard_map/ppermute | solution.py:65
  175.0 22.4 %collective-permute-start.33 = (bf16[128,1024]{1,0:T(8,128)(2,1)}, bf16[128,1024]{1,0:T(8,128)(2,1)S(1)}, u32[]{:S(2)}, u32[]{:S(2)}) collective-permute-start(bf16[128,1024]{1,0:T(8,128)(2,1)} %get-tuple-element.49.refs_4_.refs_0_), channel_id=1, source_target_pairs={{0,3},{1,0},{2,1},{3,2},{4,7},{5,4},{6,5},{7,6},{8,11},{9,8},{10,9... | collective-permute-start | bytes 786440 | tf_op jit(solution)/shard_map/ppermute | solution.py:65
  195.3 8.7 %collective-permute-start.29 = (bf16[2,64,1024]{2,1,0:T(8,128)(2,1)}, bf16[2,64,1024]{2,1,0:T(8,128)(2,1)}, u32[]{:S(2)}, u32[]{:S(2)}) collective-permute-start(bf16[2,64,1024]{2,1,0:T(8,128)(2,1)} %collective-permute-done.28.refs_4_), channel_id=1, source_target_pairs={{0,1},{1,0},{2,3},{3,2},{4,5},{5,4},{6,7},{7,6},{8,9},{9,8},{10,11... | collective-permute-start | bytes 786440 | tf_op jit(solution)/shard_map/ppermute | solution.py:264
  199.1 9.6 %collective-permute-start.35 = (bf16[2,64,1024]{2,1,0:T(8,128)(2,1)}, bf16[2,64,1024]{2,1,0:T(8,128)(2,1)}, u32[]{:S(2)}, u32[]{:S(2)}) collective-permute-start(bf16[2,64,1024]{2,1,0:T(8,128)(2,1)} %shard_map.73.refs_8_), channel_id=1, source_target_pairs={{0,8},{4,12},{8,0},{12,4},{1,9},{5,13},{9,1},{13,5},{2,10},{6,14},... | collective-permute-start | bytes 786440 | tf_op jit(solution)/shard_map/ppermute | solution.py:260
  201.5 27.1 %collective-permute-start.27 = (bf16[4,128,1024]{2,1,0:T(8,128)(2,1)}, bf16[4,128,1024]{2,1,0:T(8,128)(2,1)S(1)}, u32[]{:S(2)}, u32[]{:S(2)}) collective-permute-start(bf16[4,128,1024]{2,1,0:T(8,128)(2,1)} %copy-done.6), channel_id=1, source_target_pairs={{0,8},{4,12},{8,0},{12,4},{1,9},{5,13},{9,1},{13,5},{2,10},{6,14},... | collective-permute-start | bytes 3145736 | tf_op jit(solution)/shard_map/ppermute | solution.py:272
  202.9 27.9 %collective-permute-start.37 = (bf16[128,1024]{1,0:T(8,128)(2,1)S(1)}, bf16[128,1024]{1,0:T(8,128)(2,1)S(1)}, u32[]{:S(2)}, u32[]{:S(2)}) collective-permute-start(bf16[128,1024]{1,0:T(8,128)(2,1)S(1)} %get-tuple-element.53.refs_4_.refs_0_), channel_id=1, source_target_pairs={{0,1},{1,2},{2,3},{3,0},{4,5},{5,6},{6,7},{7,4},{8,9},{9,10},{10,1... | collective-permute-start | bytes 786440 | tf_op jit(solution)/shard_map/ppermute | solution.py:65
  204.0 27.6 %collective-permute-start.38 = (bf16[128,1024]{1,0:T(8,128)(2,1)S(1)}, bf16[128,1024]{1,0:T(8,128)(2,1)S(1)}, u32[]{:S(2)}, u32[]{:S(2)}) collective-permute-start(bf16[128,1024]{1,0:T(8,128)(2,1)S(1)} %get-tuple-element.53.refs_4_.refs_0_), channel_id=1, source_target_pairs={{0,2},{1,3},{2,0},{3,1},{4,6},{5,7},{6,4},{7,5},{8,10},{9,11},{10,... | collective-permute-start | bytes 786440 | tf_op jit(solution)/shard_map/ppermute | solution.py:65
  208.7 24.1 %collective-permute-start.39 = (bf16[128,1024]{1,0:T(8,128)(2,1)S(1)}, bf16[128,1024]{1,0:T(8,128)(2,1)S(1)}, u32[]{:S(2)}, u32[]{:S(2)}) collective-permute-start(bf16[128,1024]{1,0:T(8,128)(2,1)S(1)} %get-tuple-element.53.refs_4_.refs_0_), channel_id=1, source_target_pairs={{0,3},{1,0},{2,1},{3,2},{4,7},{5,4},{6,5},{7,6},{8,11},{9,8},{10,9... | collective-permute-start | bytes 786440 | tf_op jit(solution)/shard_map/ppermute | solution.py:65
  210.9 25.7 %collective-permute-start.36 = (bf16[2,64,1024]{2,1,0:T(8,128)(2,1)}, bf16[2,64,1024]{2,1,0:T(8,128)(2,1)S(1)}, u32[]{:S(2)}, u32[]{:S(2)}) collective-permute-start(bf16[2,64,1024]{2,1,0:T(8,128)(2,1)} %collective-permute-done.35.refs_4_), channel_id=1, source_target_pairs={{0,1},{1,0},{2,3},{3,2},{4,5},{5,4},{6,7},{7,6},{8,9},{9,8},{10,11... | collective-permute-start | bytes 786440 | tf_op jit(solution)/shard_map/ppermute | solution.py:264
  228.6 26.1 %collective-permute-start.34 = (bf16[4,128,1024]{2,1,0:T(8,128)(2,1)S(1)}, bf16[4,128,1024]{2,1,0:T(8,128)(2,1)S(1)}, u32[]{:S(2)}, u32[]{:S(2)}) collective-permute-start(bf16[4,128,1024]{2,1,0:T(8,128)(2,1)S(1)} %get-tuple-element.54.refs_0_), channel_id=1, source_target_pairs={{0,8},{4,12},{8,0},{12,4},{1,9},{5,13},{9,1},{13,5},{2,10},{6,14},... | collective-permute-start | bytes 3145736 | tf_op jit(solution)/shard_map/ppermute | solution.py:272
  230.9 24.4 %collective-permute-start.43 = (bf16[128,1024]{1,0:T(8,128)(2,1)S(1)}, bf16[128,1024]{1,0:T(8,128)(2,1)S(1)}, u32[]{:S(2)}, u32[]{:S(2)}) collective-permute-start(bf16[128,1024]{1,0:T(8,128)(2,1)S(1)} %get-tuple-element.57.refs_4_.refs_0_), channel_id=1, source_target_pairs={{0,1},{1,2},{2,3},{3,0},{4,5},{5,6},{6,7},{7,4},{8,9},{9,10},{10,1... | collective-permute-start | bytes 786440 | tf_op jit(solution)/shard_map/ppermute | solution.py:65
  231.5 23.8 %collective-permute-start.44 = (bf16[128,1024]{1,0:T(8,128)(2,1)S(1)}, bf16[128,1024]{1,0:T(8,128)(2,1)S(1)}, u32[]{:S(2)}, u32[]{:S(2)}) collective-permute-start(bf16[128,1024]{1,0:T(8,128)(2,1)S(1)} %get-tuple-element.57.refs_4_.refs_0_), channel_id=1, source_target_pairs={{0,2},{1,3},{2,0},{3,1},{4,6},{5,7},{6,4},{7,5},{8,10},{9,11},{10,... | collective-permute-start | bytes 786440 | tf_op jit(solution)/shard_map/ppermute | solution.py:65
  232.8 22.5 %collective-permute-start.45 = (bf16[128,1024]{1,0:T(8,128)(2,1)S(1)}, bf16[128,1024]{1,0:T(8,128)(2,1)S(1)}, u32[]{:S(2)}, u32[]{:S(2)}) collective-permute-start(bf16[128,1024]{1,0:T(8,128)(2,1)S(1)} %get-tuple-element.57.refs_4_.refs_0_), channel_id=1, source_target_pairs={{0,3},{1,0},{2,1},{3,2},{4,7},{5,4},{6,5},{7,6},{8,11},{9,8},{10,9... | collective-permute-start | bytes 786440 | tf_op jit(solution)/shard_map/ppermute | solution.py:65
  236.6 23.4 %collective-permute-start.41 = (bf16[2,64,1024]{2,1,0:T(8,128)(2,1)S(1)}, bf16[2,64,1024]{2,1,0:T(8,128)(2,1)}, u32[]{:S(2)}, u32[]{:S(2)}) collective-permute-start(bf16[2,64,1024]{2,1,0:T(8,128)(2,1)S(1)} %shard_map.76.refs_8_), channel_id=1, source_target_pairs={{0,8},{4,12},{8,0},{12,4},{1,9},{5,13},{9,1},{13,5},{2,10},{6,14},... | collective-permute-start | bytes 786440 | tf_op jit(solution)/shard_map/ppermute | solution.py:260
  257.8 9.1 %collective-permute-start.47 = (bf16[2,64,1024]{2,1,0:T(8,128)(2,1)}, bf16[2,64,1024]{2,1,0:T(8,128)(2,1)}, u32[]{:S(2)}, u32[]{:S(2)}) collective-permute-start(bf16[2,64,1024]{2,1,0:T(8,128)(2,1)} %shard_map.79.refs_8_), channel_id=1, source_target_pairs={{0,8},{4,12},{8,0},{12,4},{1,9},{5,13},{9,1},{13,5},{2,10},{6,14},... | collective-permute-start | bytes 786440 | tf_op jit(solution)/shard_map/ppermute | solution.py:260
  260.0 9.4 %collective-permute-start.42 = (bf16[2,64,1024]{2,1,0:T(8,128)(2,1)}, bf16[2,64,1024]{2,1,0:T(8,128)(2,1)}, u32[]{:S(2)}, u32[]{:S(2)}) collective-permute-start(bf16[2,64,1024]{2,1,0:T(8,128)(2,1)} %collective-permute-done.41.refs_4_), channel_id=1, source_target_pairs={{0,1},{1,0},{2,3},{3,2},{4,5},{5,4},{6,7},{7,6},{8,9},{9,8},{10,11... | collective-permute-start | bytes 786440 | tf_op jit(solution)/shard_map/ppermute | solution.py:264
  260.2 29.0 %collective-permute-start.40 = (bf16[4,128,1024]{2,1,0:T(8,128)(2,1)S(1)}, bf16[4,128,1024]{2,1,0:T(8,128)(2,1)S(1)}, u32[]{:S(2)}, u32[]{:S(2)}) collective-permute-start(bf16[4,128,1024]{2,1,0:T(8,128)(2,1)S(1)} %get-tuple-element.58.refs_0_), channel_id=1, source_target_pairs={{0,8},{4,12},{8,0},{12,4},{1,9},{5,13},{9,1},{13,5},{2,10},{6,14},... | collective-permute-start | bytes 3145736 | tf_op jit(solution)/shard_map/ppermute | solution.py:272
  266.9 22.9 %collective-permute-start.48 = (bf16[2,64,1024]{2,1,0:T(8,128)(2,1)}, bf16[2,64,1024]{2,1,0:T(8,128)(2,1)S(1)}, u32[]{:S(2)}, u32[]{:S(2)}) collective-permute-start(bf16[2,64,1024]{2,1,0:T(8,128)(2,1)} %collective-permute-done.47.refs_4_), channel_id=1, source_target_pairs={{0,1},{1,0},{2,3},{3,2},{4,5},{5,4},{6,7},{7,6},{8,9},{9,8},{10,11... | collective-permute-start | bytes 786440 | tf_op jit(solution)/shard_map/ppermute | solution.py:264
  284.9 26.9 %collective-permute-start.46 = (bf16[4,128,1024]{2,1,0:T(8,128)(2,1)}, bf16[4,128,1024]{2,1,0:T(8,128)(2,1)}, u32[]{:S(2)}, u32[]{:S(2)}) collective-permute-start(bf16[4,128,1024]{2,1,0:T(8,128)(2,1)} %get-tuple-element.62.refs_0_), channel_id=1, source_target_pairs={{0,8},{4,12},{8,0},{12,4},{1,9},{5,13},{9,1},{13,5},{2,10},{6,14},... | collective-permute-start | bytes 3145736 | tf_op jit(solution)/shard_map/ppermute | solution.py:272
  301.7 30.1 %collective-permute-start.49 = (bf16[4,128,1024]{2,1,0:T(8,128)(2,1)}, bf16[4,128,1024]{2,1,0:T(8,128)(2,1)S(1)}, u32[]{:S(2)}, u32[]{:S(2)}) collective-permute-start(bf16[4,128,1024]{2,1,0:T(8,128)(2,1)} %get-tuple-element.66.refs_0_), channel_id=1, source_target_pairs={{0,8},{4,12},{8,0},{12,4},{1,9},{5,13},{9,1},{13,5},{2,10},{6,14},... | collective-permute-start | bytes 3145736 | tf_op jit(solution)/shard_map/ppermute | solution.py:272
  (94 other events, 773.1 us)
